TPU v7x, 128 devices: a whole 4x4x4 slice. The times are simulated.
128 devices in a mesh: fsdp: 16 (over y_hi, x, core), ctx: 2 (over y_lo), tp: 4 (over z).
Axes of the slice: x: 4, y: 4 (y_hi: 2, y_lo: 2; y = y_hi * 2 + y_lo), z: 4, core: 2. Of those that a mesh axis runs over, the one named last changes fastest.
Arguments:
- tokens: bfloat16 [4096, 2560], P(('fsdp', 'ctx')), may hold values from -6 to 6
- cotangent: bfloat16 [4096, 2560], P(('fsdp', 'ctx')), may hold values from -6 to 6
- segments: int32 [4096], P('fsdp'), may hold values from 0 to 3, as said below
- owner: int32 [2560], replicated, may hold values from 0 to 15, as said below
- master: float32 [3840, 27904], P(('fsdp', 'ctx'), 'tp'), may hold values from -0.355756237 to 0.355756237
- moment_one: float32 [3840, 27904], P(('fsdp', 'ctx'), 'tp'), may hold values from -960 to 960
- moment_two: float32 [3840, 27904], P(('fsdp', 'ctx'), 'tp'), may hold values from 368.64 to 409600
- gains: float32 [2, 2560], replicated, may hold values from 0.5 to 1.5
- gain_one: float32 [2, 2560], replicated, may hold values from -768 to 768
- gain_two: float32 [2, 2560], replicated, may hold values from 6144 to 147456
Outputs:
- output: bfloat16 [4096, 2560], P(('fsdp', 'ctx'))
- grad_tokens: bfloat16 [4096, 2560], P(('fsdp', 'ctx'))
- new_master: float32 [3840, 27904], P(('fsdp', 'ctx'), 'tp')
- new_moment_one: float32 [3840, 27904], P(('fsdp', 'ctx'), 'tp')
- new_moment_two: float32 [3840, 27904], P(('fsdp', 'ctx'), 'tp')
- new_gains: float32 [2, 2560], replicated
- new_gain_one: float32 [2, 2560], replicated
- new_gain_two: float32 [2, 2560], replicated
Inputs may be any that keep to these rules, and one draw needn't show every extreme that they name: `segments`: in each sequence of 256 tokens the numbers start at 0 and never fall. `owner`: each index of fsdp is named at most 240 times, and one is named exactly 240 times.
All inputs are finite; a program needn't handle non-finite values.
Results may differ from a plain program's by a relative error of at most 0.014.
The roundings to bfloat16 on the way count: a program that leaves them out, or rounds other values in their place, can miss the bound.
Values may be sent and summed in bfloat16 or wider, within the bound.
No kernel may reach another device: no remote copies, remote signals or barrier semaphores. Data moves between devices by JAX's collectives and lax.ppermute only.
A program may use at most 384 MiB of HBM per device.

v0:
```python
import jax
import jax.numpy as jnp
from jax import lax
from jax.sharding import PartitionSpec as P

H = 32
KVH = 8
HD = 80
FF = 7168
STEP = 5


EPS_NORM = 1e-05
EPS_ADAM = 1e-08
THETA = 1000000.0
BETA = 0.5
LEARN = 0.05
LEARN_GAIN = 0.2
DECAY = 0.1
NEG_BIG = -1e30


def from_behind(block, axis, distance):
    devices = range(lax.axis_size(axis))
    route = [(i - distance, i) for i in devices if i - distance in devices]
    return lax.ppermute(block, axis, route)


def contract(left, right, left_axis, right_axis):
    return lax.dot_general(
        left, right, (((left_axis,), (right_axis,)), ((), ())), preferred_element_type=jnp.float32
    )


def rms_forward(values):
    scale = lax.rsqrt(jnp.mean(values * values, axis=1, keepdims=True) + EPS_NORM)
    return (values * scale, scale)


def rms_backward(grad_out, normed, scale, gain):
    grad_normed = grad_out * gain
    inner = jnp.mean(grad_normed * normed, axis=1, keepdims=True)
    return (scale * (grad_normed - normed * inner), jnp.sum(grad_out * normed, axis=0))


def rotary_tables(positions):
    half = HD // 2
    freq = jnp.exp(-jnp.log(THETA) * (2.0 * jnp.arange(half, dtype=jnp.float32) / HD))
    angle = positions.astype(jnp.float32)[:, None] * freq[None, :]
    return (jnp.cos(angle), jnp.sin(angle))


def rotate(values, cosine, sine, heads, sign):
    half = HD // 2
    shaped = values.reshape(values.shape[0], heads, HD)
    first = shaped[:, :, :half]
    second = shaped[:, :, half:]
    turned_cos = cosine[:, None, :]
    turned_sin = sine[:, None, :] * sign
    joined = jnp.concatenate(
        [first * turned_cos - second * turned_sin, second * turned_cos + first * turned_sin], axis=2
    )
    return joined.reshape(values.shape)


def feature_table(owner, fsdp_count, capacity):
    onehot = (owner[:, None] == jnp.arange(fsdp_count, dtype=jnp.int32)[None, :]).astype(jnp.int32)
    rank = jnp.sum((jnp.cumsum(onehot, axis=0) - onehot) * onehot, axis=1)
    slot = owner * capacity + rank
    features = owner.shape[0]
    table = jnp.full((fsdp_count * capacity,), features, jnp.int32)
    return table.at[slot].set(jnp.arange(features, dtype=jnp.int32))


def attention_probs(shaped, keyed, mask):
    scores = jnp.einsum(
        "ikgd,jkd->kgij", shaped, keyed, preferred_element_type=jnp.float32
    ) * HD ** (-0.5)
    scores = jnp.where(mask[None, None], scores, NEG_BIG)
    top = jnp.max(scores, axis=3, keepdims=True)
    weight = jnp.exp(scores - top)
    return weight / jnp.sum(weight, axis=3, keepdims=True)


def adam_step(weight, first, second, grad, rate, decay):
    first_new = BETA * first + (1.0 - BETA) * grad
    second_new = BETA * second + (1.0 - BETA) * grad * grad
    correction = 1.0 - BETA**STEP
    update = first_new / correction / (jnp.sqrt(second_new / correction) + EPS_ADAM)
    return (weight - rate * (update + decay * weight), first_new, second_new)


def shards(
    tokens, cotangent, segments, owner, master, moment_one, moment_two, gains, gain_one, gain_two
):
    fsdp_count = lax.axis_size("fsdp")
    ctx_count = lax.axis_size("ctx")
    tp_count = lax.axis_size("tp")
    slots_dev = master.shape[0]
    capacity = slots_dev * ctx_count
    width = master.shape[1]
    model_width = tokens.shape[1]
    rows = tokens.shape[0]
    query_width = H * HD // tp_count
    kv_width = KVH * HD // tp_count
    ff_width = FF // tp_count
    heads = H // tp_count
    kv_heads = KVH // tp_count
    group = H // KVH
    gate_start = query_width + 2 * kv_width
    out_start = gate_start + 2 * ff_width
    down_start = out_start + query_width
    slot_feature = feature_table(owner, fsdp_count, capacity)
    master_low = master.astype(jnp.bfloat16)

    def unpack(carry, piece):
        return carry.at[slot_feature].set(piece, mode="drop")

    empty = jnp.zeros((model_width, width), jnp.bfloat16)
    weights = unpack(empty, lax.all_gather(master_low, ("fsdp", "ctx"), axis=0, tiled=True))
    place = lax.axis_index("ctx")
    position = place * rows + jnp.arange(rows, dtype=jnp.int32)
    cosine, sine = rotary_tables(position)
    key_position = (place - 1) * rows + jnp.arange(2 * rows, dtype=jnp.int32)
    query_segment = lax.dynamic_slice_in_dim(segments, place * rows, rows, 0)
    key_segment = jnp.take(segments, jnp.maximum(key_position, 0), axis=0)
    mask = (
        (query_segment[:, None] == key_segment[None, :])
        & (key_position[None, :] <= position[:, None])
        & (key_position[None, :] >= 0)
    )
    inputs = tokens.astype(jnp.float32)
    normed_one, scale_one = rms_forward(inputs)
    xn_one = (normed_one * gains[0]).astype(jnp.bfloat16)
    projected = jnp.dot(xn_one, weights[:, :gate_start], preferred_element_type=jnp.float32)
    query = rotate(projected[:, :query_width], cosine, sine, heads, 1.0).astype(jnp.bfloat16)
    key_local = rotate(
        projected[:, query_width : query_width + kv_width], cosine, sine, kv_heads, 1.0
    ).astype(jnp.bfloat16)
    value_local = projected[:, query_width + kv_width :].astype(jnp.bfloat16)
    key_prev, value_prev = from_behind((key_local, value_local), "ctx", 1)
    keyed = jnp.concatenate([key_prev, key_local], axis=0).reshape(2 * rows, kv_heads, HD)
    valued = jnp.concatenate([value_prev, value_local], axis=0).reshape(2 * rows, kv_heads, HD)
    shaped = query.reshape(rows, kv_heads, group, HD)
    probs_low = attention_probs(shaped, keyed, mask).astype(jnp.bfloat16)
    attended = jnp.einsum("kgij,jkd->ikgd", probs_low, valued, preferred_element_type=jnp.float32)
    attended_low = attended.reshape(rows, query_width).astype(jnp.bfloat16)
    branch = lax.psum(contract(attended_low, weights[:, out_start:down_start], 1, 1), "tp")
    hidden = inputs + branch
    normed_two, scale_two = rms_forward(hidden)
    xn_two = (normed_two * gains[1]).astype(jnp.bfloat16)
    gate_up = jnp.dot(xn_two, weights[:, gate_start:out_start], preferred_element_type=jnp.float32)
    gate = gate_up[:, :ff_width]
    up = gate_up[:, ff_width:]
    act = (jax.nn.silu(gate) * up).astype(jnp.bfloat16)
    mlp = lax.psum(contract(act, weights[:, down_start:], 1, 1).astype(jnp.bfloat16), "tp").astype(
        jnp.float32
    )
    output = (hidden + mlp).astype(jnp.bfloat16)
    weights = unpack(empty, lax.all_gather(master_low, ("fsdp", "ctx"), axis=0, tiled=True))
    grad_act = jnp.dot(cotangent, weights[:, down_start:], preferred_element_type=jnp.float32)
    sigmoid = jax.nn.sigmoid(gate)
    grad_gate = grad_act * up * sigmoid * (1.0 + gate * (1.0 - sigmoid))
    grad_up = grad_act * (gate * sigmoid)
    grad_gate_up = jnp.concatenate([grad_gate, grad_up], axis=1).astype(jnp.bfloat16)
    grad_xn_two = lax.psum(contract(grad_gate_up, weights[:, gate_start:out_start], 1, 1), "tp")
    grad_norm_two, gain_grad_two = rms_backward(grad_xn_two, normed_two, scale_two, gains[1])
    grad_hidden = cotangent.astype(jnp.float32) + grad_norm_two
    grad_branch = grad_hidden.astype(jnp.bfloat16)
    grad_attended = jnp.dot(
        grad_branch, weights[:, out_start:down_start], preferred_element_type=jnp.float32
    ).astype(jnp.bfloat16)
    shaped_grad = grad_attended.reshape(rows, kv_heads, group, HD)
    probs = attention_probs(shaped, keyed, mask)
    grad_probs = jnp.einsum(
        "ikgd,jkd->kgij", shaped_grad, valued, preferred_element_type=jnp.float32
    )
    inner = jnp.sum(probs * grad_probs, axis=3, keepdims=True)
    grad_scores = (probs * (grad_probs - inner)).astype(jnp.bfloat16)
    factor = HD ** (-0.5)
    grad_query = (
        jnp.einsum("kgij,jkd->ikgd", grad_scores, keyed, preferred_element_type=jnp.float32)
        * factor
    )
    grad_keys = (
        jnp.einsum("kgij,ikgd->jkd", grad_scores, shaped, preferred_element_type=jnp.float32)
        * factor
    )
    grad_values = jnp.einsum(
        "kgij,ikgd->jkd",
        probs.astype(jnp.bfloat16),
        shaped_grad,
        preferred_element_type=jnp.float32,
    )
    grad_keys = grad_keys.reshape(2 * rows, kv_width)
    grad_values = grad_values.reshape(2 * rows, kv_width)
    back_key, back_value = (
        from_behind(grad_keys[:rows].astype(jnp.bfloat16), "ctx", -1).astype(jnp.float32),
        from_behind(grad_values[:rows].astype(jnp.bfloat16), "ctx", -1).astype(jnp.float32),
    )
    grad_key = grad_keys[rows:] + back_key
    grad_value = grad_values[rows:] + back_value
    grad_qkv = jnp.concatenate(
        [
            rotate(grad_query.reshape(rows, query_width), cosine, sine, heads, -1.0),
            rotate(grad_key, cosine, sine, kv_heads, -1.0),
            grad_value,
        ],
        axis=1,
    ).astype(jnp.bfloat16)
    grad_xn_one = lax.psum(contract(grad_qkv, weights[:, :gate_start], 1, 1), "tp")
    grad_norm_one, gain_grad_one = rms_backward(grad_xn_one, normed_one, scale_one, gains[0])
    grad_tokens = (grad_hidden + grad_norm_one).astype(jnp.bfloat16)
    lefts = (xn_one, xn_two, grad_branch, cotangent)
    rights = (grad_qkv, grad_gate_up, attended_low, act)
    pieces = []
    for left, right in zip(lefts, rights):
        chosen = jnp.take(left, slot_feature, axis=1, mode="fill", fill_value=0)
        pieces.append(contract(chosen, right, 0, 0))
    unit_terms = jnp.concatenate(pieces, axis=1)
    total_slots = unit_terms.shape[0]
    received = lax.all_to_all(
        unit_terms.astype(jnp.bfloat16), ("fsdp", "ctx"), split_axis=0, concat_axis=0, tiled=True
    ).astype(unit_terms.dtype)
    grad_master = jnp.sum(received.reshape(total_slots // slots_dev, slots_dev, width), axis=0)
    grad_gains = lax.psum(jnp.stack([gain_grad_one, gain_grad_two]), ("fsdp", "ctx"))
    local_feature = lax.dynamic_slice_in_dim(
        slot_feature, lax.axis_index(("fsdp", "ctx")) * slots_dev, slots_dev, 0
    )
    valid = (local_feature < model_width)[:, None]
    new_master, new_one, new_two = adam_step(
        master, moment_one, moment_two, grad_master, LEARN, DECAY
    )
    zero = jnp.zeros_like(master)
    new_gains, new_gain_one, new_gain_two = adam_step(
        gains, gain_one, gain_two, grad_gains, LEARN_GAIN, 0.0
    )
    return (
        output,
        grad_tokens,
        jnp.where(valid, new_master, zero),
        jnp.where(valid, new_one, zero),
        jnp.where(valid, new_two, zero),
        new_gains,
        new_gain_one,
        new_gain_two,
    )


def solution(mesh):
    in_specs = (
        P(("fsdp", "ctx"), None),
        P(("fsdp", "ctx"), None),
        P("fsdp"),
        P(),
        P(("fsdp", "ctx"), "tp"),
        P(("fsdp", "ctx"), "tp"),
        P(("fsdp", "ctx"), "tp"),
        P(),
        P(),
        P(),
    )
    out_specs = (
        P(("fsdp", "ctx"), None),
        P(("fsdp", "ctx"), None),
        P(("fsdp", "ctx"), "tp"),
        P(("fsdp", "ctx"), "tp"),
        P(("fsdp", "ctx"), "tp"),
        P(),
        P(),
        P(),
    )
    return jax.shard_map(shards, mesh=mesh, in_specs=in_specs, out_specs=out_specs, check_vma=False)
```

profile of v0, /device:TPU:1, one launch (start us, length us, event | category | flops | bytes accessed | tf_op | source)
XLA Modules:
  0.0 1949.4 jit_solution(11996317496216322583)
XLA Ops:
  7.2 3.3 convert_element_type.104
  10.7 4.6 reduce-window.6
  16.0 1.9 gather_fusion
  18.2 9.9 scatter_custom_fusion
  28.1 5.1 sort
  34.2 273.3 %all-gather.2.cloned.1.call-done = bf16[3840,6976]{1,0:T(8,128)(2,1)} async-done(((bf16[120,6976]{1,0:T(8,128)(2,1)}), bf16[3840,6976]{1,0:T(8,128)(2,1)}) %all-gather.2.cloned.1.call-update) | async-done | bytes 53575696 | tf_op jit(solution)/shard_map/all_gather | solution.py:120
  307.5 376.1 %scatter_custom_fusion.1 = bf16[2560,6976]{1,0:T(8,128)(2,1)} fusion(s32[3840]{0:T(1024)S(1)} %get-tuple-element.9, bf16[3840,6976]{1,0:T(8,128)(2,1)} %all-gather.2.cloned.1.call-done, s32[4096]{0:T(1024)S(1)} %pad_clamp_fusion.1, bf16[]{:T(256)} %constant.42.clone.1), kind=kCustom, calls=%fused_computation.10 | custom fusion | bytes 35717632 | tf_op jit(solution)/shard_map/scatter | solution.py:117
  683.7 4.6 fusion.17
  688.4 2.3 collective-permute-start
  690.7 1.3 collective-permute-start.1
  693.2 1.5 fusion.88
  695.5 4.9 fusion.25
  701.2 8.7 gather_fusion.1
  709.8 8.7 gather_fusion.4
  718.6 31.5 %all-reduce.5.cloned.1.call-done = f32[128,2560]{1,0:T(8,128)} async-done(((f32[128,2560]{1,0:T(8,128)}), f32[128,2560]{1,0:T(8,128)}) %all-reduce.5.cloned.1.call-update) | async-done | bytes 1310736 | tf_op jit(solution)/shard_map/psum | solution.py:148
  750.1 1.6 multiply_reduce_fusion.2
  752.8 14.1 fusion.9
  766.9 1.4 copy.38
  768.3 8.9 multiply_convert_fusion.3
  777.2 15.4 fusion.7
  792.6 8.6 gather_fusion.2
  801.3 9.3 convolution_convert_fusion.1
  810.6 14.9 convolution_convert_fusion
  825.5 15.8 all-reduce.9.cloned.1.call-done
  841.3 1.8 multiply_reduce_fusion
  844.4 3.4 fusion.46
  848.0 2.2 convolution_bitcast_fusion.1
  850.2 1.7 multiply_reduce_fusion.3
  854.0 1.4 copy.39
  855.4 1.5 slice.208
  856.9 1.3 collective-permute-start.3
  858.2 1.5 slice.209
  859.7 1.3 collective-permute-start.2
  861.0 8.7 gather_fusion.3
  869.6 3.3 broadcast_select_fusion.2
  874.0 3.9 convolution_convert_fusion.3
  879.6 4.8 convolution_convert_fusion.2
  884.4 10.2 copy.53
  894.7 95.7 %concatenate.52 = bf16[32,120,6976]{2,1,0:T(8,128)(2,1)} concatenate(bf16[32,120,960]{2,1,0:T(8,128)(2,1)} %bitcast.131, bf16[32,120,3584]{2,1,0:T(8,128)(2,1)} %bitcast.129, bf16[32,120,640]{2,1,0:T(8,128)(2,1)} %convolution_convert_fusion.3, bf16[32,120,1792]{2,1,0:T(8,128)(2,1)} %bitcast.130), dimensions={2} | concatenate | bytes 107151360 | tf_op jit(solution)/shard_map/concatenate | solution.py:220
  990.4 11.2 all-to-all-start
  1001.6 5.5 fusion.15
  1007.5 7.9 fusion.19
  1015.4 39.2 %all-reduce.11.cloned.1.call-done = f32[128,2560]{1,0:T(8,128)} async-done(((f32[128,2560]{1,0:T(8,128)}), f32[128,2560]{1,0:T(8,128)}) %all-reduce.11.cloned.1.call-update) | async-done | bytes 1310736 | tf_op jit(solution)/shard_map/psum | solution.py:211
  1054.6 1.8 fusion.44
  1056.4 856.7 %psum.39 = f32[2,2560]{1,0:T(2,128)S(1)} all-reduce(f32[2,2560]{1,0:T(2,128)S(1)} %pad_maximum_fusion.12), channel_id=1, replica_groups=mesh['fsdp'=16,'ctx'=2,'tp'=4] {'fsdp','ctx'}, use_global_device_ids=true, to_apply=%region_19.21 | all-reduce | flops 5120 | bytes 40960 | tf_op jit(solution)/shard_map/psum | solution.py:226
  1913.8 3.6 fusion.43
  1917.4 17.4 convert_reduce_fusion
  1934.8 7.9 broadcast_select_fusion
  (130 shorter events, 13.0 us)
Async XLA Ops:
  7.2 3.5 copy-start.16
  7.2 8.7 copy-start
  7.2 300.3 %all-gather.2.cloned.1.call-start = ((), (), s32[]{:S(2)}) async-start(), calls=%async_computation.1 | async-start | bytes 55756800 | tf_op jit(solution)/shard_map/all_gather | solution.py:120
  10.6 22.8 %copy-start.17 = (f32[2,2560]{1,0:T(2,128)S(1)}, f32[2,2560]{1,0:T(2,128)}, u32[]{:S(2)}) copy-start(f32[2,2560]{1,0:T(2,128)} %param.19) | copy-start | bytes 61444
  10.6 22.8 %copy-start.1 = (bf16[128,2560]{1,0:T(8,128)(2,1)S(1)}, bf16[128,2560]{1,0:T(8,128)(2,1)}, u32[]{:S(2)}) copy-start(bf16[128,2560]{1,0:T(8,128)(2,1)} %param.12) | copy-start | bytes 1966084
  10.6 739.5 %all-reduce.5.cloned.1.call-start = ((), (), s32[]{:S(2)}) async-start(), calls=%async_computation.2 | async-start | bytes 2621440 | tf_op jit(solution)/shard_map/psum | solution.py:148
  33.4 650.3 %copy-start.14 = (f32[2560]{0:T(1024)}, f32[2560]{0:T(1024)S(1)}, u32[]{:S(2)}) copy-start(f32[2560]{0:T(1024)S(1)} %get-tuple-element.16) | copy-start | bytes 30724
  33.6 650.0 %copy-start.24 = (f32[128]{0:T(128)}, f32[128]{0:T(128)S(1)}, u32[]{:S(2)}) copy-start(f32[128]{0:T(128)S(1)} %add_rsqrt_fusion.1) | copy-start | bytes 1540
  33.8 660.9 %copy-start.21 = (pred[128,256]{0,1:T(8,128)(4,1)}, pred[128,256]{0,1:T(8,128)(4,1)S(1)}, u32[]{:S(2)}) copy-start(pred[128,256]{0,1:T(8,128)(4,1)S(1)} %and_and_fusion) | copy-start | bytes 98308
  688.4 6.4 collective-permute-start
  690.7 2.5 collective-permute-start.1
  692.1 3.4 copy-start.8
  693.2 7.2 copy-start.12
  694.7 5.7 copy-start.19
  695.5 5.3 copy-start.3
  700.4 140.9 %all-reduce.9.cloned.1.call-start = ((), (), s32[]{:S(2)}) async-start(), calls=%async_computation.4 | async-start | bytes 2621440 | tf_op jit(solution)/shard_map/psum | solution.py:166
  751.9 0.8 copy-start.6
  801.3 9.3 copy-start.10
  841.3 1.8 copy-start.2
  843.6 0.8 copy-start.5
  844.4 3.6 copy-start.9
  844.4 3.6 copy-start.13
  847.8 2.4 copy-start.20
  850.2 1.7 copy-start.7
  856.9 21.9 %collective-permute-start.3 = (bf16[128,160]{0,1:T(8,128)(2,1)}, bf16[128,160]{0,1:T(8,128)(2,1)}, u32[]{:S(2)}, u32[]{:S(2)}) collective-permute-start(bf16[128,160]{0,1:T(8,128)(2,1)} %bitcast.39), channel_id=1, source_target_pairs={{4,0},{5,1},{6,2},{7,3},{12,8},{13,9},{14,10},{15,11},{20,16},{21,... | collective-permute-start | bytes 122888 | tf_op jit(solution)/shard_map/ppermute | solution.py:26
  859.7 18.2 collective-permute-start.2
  874.0 4.0 slice-start
  874.0 4.8 slice-start.1
  874.0 5.6 copy-start.4
  990.4 927.1 %all-to-all-start = ((bf16[32,120,6976]{2,1,0:T(8,128)(2,1)}), bf16[32,120,6976]{2,1,0:T(8,128)(2,1)}, u32[]{:S(2)}, u32[]{:S(2)}) async-start(bf16[32,120,6976]{2,1,0:T(8,128)(2,1)} %concatenate.52), calls=%async_computation | async-start | bytes 108134400 | tf_op jit(solution)/shard_map/all_to_all | solution.py:222
  1001.6 5.9 copy-start.11
  1001.6 53.0 %all-reduce.11.cloned.1.call-start = ((), (), s32[]{:S(2)}) async-start(), calls=%async_computation.5 | async-start | bytes 2621440 | tf_op jit(solution)/shard_map/psum | solution.py:211
  1007.1 906.7 %all-reduce.7.cloned.1.call-start = ((), (), s32[]{:S(2)}) async-start(), calls=%async_computation.3 | async-start | bytes 1310720 | tf_op jit(solution)/shard_map/psum | solution.py:156
  1007.4 47.2 %copy-start.15 = (f32[2560]{0:T(1024)S(1)}, f32[2560]{0:T(1024)}, u32[]{:S(2)}) copy-start(f32[2560]{0:T(1024)} %copy-done.14) | copy-start | bytes 30724
  1007.5 47.2 %copy-start.25 = (f32[128]{0:T(128)S(1)}, f32[128]{0:T(128)}, u32[]{:S(2)}) copy-start(f32[128]{0:T(128)} %copy-done.24) | copy-start | bytes 1540
  1007.5 905.6 %copy-start.18 = (f32[2,2560]{1,0:T(2,128)S(1)}, f32[2,2560]{1,0:T(2,128)}, u32[]{:S(2)}) copy-start(f32[2,2560]{1,0:T(2,128)} %param.19) | copy-start | bytes 61444
  1007.5 905.6 %copy-start.22 = (f32[2,2560]{1,0:T(2,128)S(1)}, f32[2,2560]{1,0:T(2,128)}, u32[]{:S(2)}) copy-start(f32[2,2560]{1,0:T(2,128)} %param.20) | copy-start | bytes 61444
  1007.5 905.6 %copy-start.23 = (f32[2,2560]{1,0:T(2,128)S(1)}, f32[2,2560]{1,0:T(2,128)}, u32[]{:S(2)}) copy-start(f32[2,2560]{1,0:T(2,128)} %param.21) | copy-start | bytes 61444
Sparse Core Ops, SparseCore 0:
  10.7 296.7 all-gather.1
  700.6 49.5 all-reduce.4
  792.8 48.4 all-reduce.8
  1007.3 47.3 all-reduce.10
  1057.4 43.8 all-reduce.6
where the time goes:
time: 1950 us
  blocking collectives  857 us (44%)
  local copies, waits for them, and re-layouts  538 us (28%)
  waiting for transfers between devices  361 us (19%)
  matrix products  106 us (5%)
  other arithmetic  56 us (3%)
    psum x1, blocking collectives, shards(): lax.psum(jnp.stack([gain_grad_one, gain_grad_two]), ('fsdp', 'ctx'))  857 us
    scatter x2, local copies, waits for them, and re-layouts, unpack(): return carry.at[slot_feature].set(piece, mode='drop')  376 us
    all_gather x1, waiting for transfers between devices, shards(): lax.all_gather(master_low, ('fsdp', 'ctx'), axis=0, tiled=True)  273 us
    concatenate x2, local copies, waits for them, and re-layouts, shards(): unit_terms = jnp.concatenate(pieces, axis=1)  106 us
    dot_general x8, matrix products, contract(): lax.dot_general(left, right, (((left_axis,), (right_axis,)), ((), ())), p...  66.7 us
    psum x1, waiting for transfers between devices, shards(): lax.psum(contract(grad_qkv, weights[:, :gate_start], 1, 1), 'tp')  39.2 us
  transfers between devices with their start and end apart: 10, of which 5 were waited for; matrix products, arithmetic and copies ran while one was open for 6% of the time, Pallas kernels for 0%

commit v1 on v0

v1 whole, which is shorter than its diff:
```python
import functools

import jax
import jax.numpy as jnp
from jax import lax
from jax.experimental import pallas as pl
from jax.experimental.pallas import tpu as pltpu
from jax.sharding import Mesh
from jax.sharding import PartitionSpec as P

HD = 80
STEP = 5
D = 2560
CAP = 240
HALF = 120
SEQ = 256
RING = 4

EPS_NORM = 1e-05
EPS_ADAM = 1e-08
THETA = 1000000.0
BETA = 0.5
LEARN = 0.05
LEARN_GAIN = 0.2
DECAY = 0.1
NEG_BIG = -1e30

X = "x"
Y = ("yh", "yl")
OFFSETS = (0, -1, 1, 2)
LOW = jnp.bfloat16
F32 = jnp.float32

HEADS = 4
QW = 320
KW = 80
FW = 896
ATTN = 896
CUT = 512
FFN = 3 * FW
FFN_CUT = 1408
WIDE = ATTN + FFN
WIDE_CUT = 1792
MAP = (
    (0, 320, QW),
    (640, 640, KW),
    (800, 720, KW),
    (960, 1792, FW),
    (2752, 2688, FW),
    (4544, 0, QW),
    (5184, 896, FW),
)
PIECES = 8
BLK = 4 * HALF
LANES = 512
VMEM = 60 * 1024 * 1024


def dot(left, right, left_axis, right_axis):
    return lax.dot_general(
        left, right, (((left_axis,), (right_axis,)), ((), ())), preferred_element_type=F32
    )


def move(block, axis, distance):
    route = [(i, (i + distance) % RING) for i in range(RING)]
    return lax.ppermute(block, axis, route)


def swap_core(block):
    return lax.ppermute(block, "core", [(0, 1), (1, 0)])


def swap_sequences(block):
    return lax.ppermute(block, ("core", "yl"), [(0, 0), (1, 2), (2, 1), (3, 3)])


def near(block, axis):
    return move(block, axis, 1), move(block, axis, -1)


def far(back, ahead, axis):
    return move(back, axis, 1), move(ahead, axis, -1)


def halves(back, ahead, axis, cut):
    return far(back[:, :cut], ahead[:, cut:], axis)


def slot_ids(x, y):
    offsets = jnp.array(OFFSETS, jnp.int32)
    every = jnp.arange(RING, dtype=jnp.int32)
    rows = jnp.arange(HALF, dtype=jnp.int32)

    def slots(xx, yy, core):
        return (((yy // 2) * RING + xx) * 2 + core) * CAP + (yy % 2) * HALF

    first = slots(((x + offsets) % RING)[None, :, None], every[:, None, None], 0) + rows
    second = slots(every[:, None, None], ((y + offsets) % RING)[None, :, None], 1) + rows
    ids = jnp.concatenate([first, second], axis=0).reshape(PIECES, 1, BLK)
    return jnp.pad(ids, ((0, 0), (0, 0), (0, LANES - BLK)), constant_values=-1)


def three_parts(values):
    high = lax.reduce_precision(values, 8, 7)
    rest = values - high
    middle = lax.reduce_precision(rest, 8, 7)
    return jnp.concatenate([high, middle, rest - middle], axis=0).astype(LOW)


def whole():
    return pl.BlockSpec(memory_space=pltpu.VMEM)


def hbm():
    return pl.BlockSpec(memory_space=pl.ANY)


def smem():
    return pl.BlockSpec(memory_space=pltpu.SMEM)


def cost(flops, size):
    return pl.CostEstimate(flops=flops, bytes_accessed=size, transcendentals=0)


def pack_kernel(meta_ref, master_ref, own_ref, send_ref):
    is_low = meta_ref[0] == 0
    valid = lax.broadcasted_iota(jnp.int32, (HALF, 1), 0) < meta_ref[4]
    blank = jnp.zeros((HALF, ATTN - 800), LOW)
    own_ref[:, 800:ATTN] = blank
    send_ref[:, 800:ATTN] = blank
    for start, at, width in MAP:
        low = jnp.where(valid, master_ref[:, start : start + width], 0.0)
        high = jnp.where(valid, master_ref[:, start + width : start + 2 * width], 0.0)
        own_ref[:, at : at + width] = jnp.where(is_low, low, high).astype(LOW)
        send_ref[:, at : at + width] = jnp.where(is_low, high, low).astype(LOW)


def pack(meta, master):
    return pl.pallas_call(
        pack_kernel,
        in_specs=[smem(), whole()],
        out_specs=[whole()] * 2,
        out_shape=[jax.ShapeDtypeStruct((HALF, WIDE), LOW)] * 2,
        compiler_params=pltpu.CompilerParams(vmem_limit_bytes=VMEM),
        name="pack",
    )(meta, master)


def assemble_kernel(*refs):
    for kind in range(2):
        block, back, ahead, one, two = refs[5 * kind : 5 * kind + 5]
        outs = refs[10 + 4 * kind : 14 + 4 * kind]
        for j, out in enumerate(outs):
            at = j * FW
            for k, ref in enumerate((block, back, ahead)):
                out[k * HALF : (k + 1) * HALF, :] = ref[:, at : at + FW]
            last = one if j < 2 else two
            at = at % WIDE_CUT
            out[3 * HALF :, :] = last[:, at : at + FW]


def assemble(*blocks):
    return pl.pallas_call(
        assemble_kernel,
        in_specs=[whole()] * 10,
        out_specs=[whole()] * 8,
        out_shape=[jax.ShapeDtypeStruct((BLK, FW), LOW)] * 8,
        compiler_params=pltpu.CompilerParams(vmem_limit_bytes=VMEM),
        cost_estimate=cost(0, 0),
        name="assemble",
    )(*blocks)


def place_kernel(
    meta_ref, slot_ref, ids_ref, swapped_ref, gains_ref, parts_ref, xc_ref, in_ref, cot_ref, gain_ref, rows
):
    @pl.when(pl.program_id(0) == 0)
    def _():
        at = pl.multiple_of(meta_ref[1] * 32, 32)
        tokens = swapped_ref[:128].astype(F32)
        scale = lax.rsqrt(jnp.sum(tokens * tokens, axis=1, keepdims=True) / D + EPS_NORM)
        rows[:128] = (tokens * scale * gains_ref[0:1]).astype(LOW)
        rows[128:256] = swapped_ref[128:256]
        rows[256:288] = swapped_ref[pl.ds(at, 32)]
        rows[288:320] = swapped_ref[pl.ds(128 + at, 32)]
        rows[320:] = parts_ref[...]

    place = jnp.where(slot_ref[...] == ids_ref[0], 1.0, 0.0).astype(LOW)
    placed = dot(rows[...], place, 1, 0)
    xc_ref[0] = placed[:256].astype(LOW)
    in_ref[0] = placed[256:288]
    cot_ref[0] = placed[288:320]
    gain_ref[0] = placed[320:322] + placed[322:324] + placed[324:326]


def to_slots(meta, slot, ids, swapped, gains, parts):
    def piece(rows):
        return pl.BlockSpec((1, rows, LANES), lambda p: (p, 0, 0))

    def same(shape):
        return pl.BlockSpec(shape, lambda p: (0, 0))

    return pl.pallas_call(
        place_kernel,
        grid=(PIECES,),
        in_specs=[
            smem(),
            same((D, 1)),
            pl.BlockSpec((1, 1, LANES), lambda p: (p, 0, 0)),
            same(swapped.shape),
            same((2, D)),
            same((16, D)),
        ],
        out_specs=[piece(256), piece(32), piece(32), piece(2)],
        out_shape=[
            jax.ShapeDtypeStruct((PIECES, 256, LANES), LOW),
            jax.ShapeDtypeStruct((PIECES, 32, LANES), F32),
            jax.ShapeDtypeStruct((PIECES, 32, LANES), F32),
            jax.ShapeDtypeStruct((PIECES, 2, LANES), F32),
        ],
        scratch_shapes=[pltpu.VMEM((336, D), LOW)],
        compiler_params=pltpu.CompilerParams(vmem_limit_bytes=VMEM),
        cost_estimate=cost(0, 0),
        name="to_slots",
    )(meta, slot, ids, swapped, gains, parts)


def unplace_kernel(slot_ref, ids_ref, rows_ref, out_ref):
    place = jnp.where(slot_ref[...] == ids_ref[0], 1.0, 0.0).astype(LOW)

    @pl.when(pl.program_id(0) == 0)
    def _():
        out_ref[...] = jnp.zeros_like(out_ref)

    out_ref[...] += dot(rows_ref[0], place, 1, 1)


def from_slots(rows, slot, ids):
    n = rows.shape[1]
    return pl.pallas_call(
        unplace_kernel,
        grid=(PIECES,),
        in_specs=[
            pl.BlockSpec((D, 1), lambda p: (0, 0)),
            pl.BlockSpec((1, 1, LANES), lambda p: (p, 0, 0)),
            pl.BlockSpec((1, n, LANES), lambda p: (p, 0, 0)),
        ],
        out_specs=pl.BlockSpec((n, D), lambda p: (0, 0)),
        out_shape=jax.ShapeDtypeStruct((n, D), F32),
        compiler_params=pltpu.CompilerParams(vmem_limit_bytes=VMEM),
        name="from_slots",
    )(slot, ids, rows)


def start_weights(meta_ref, refs, held, sems, cut):
    x = meta_ref[2]
    y = meta_ref[3]
    for base, at, group in ((0, y, refs[:5]), (RING, x, refs[5:])):
        for ref, offset in zip(group[:3], (0, -1, 1)):
            p = base + lax.rem(at + offset + RING, RING)
            pltpu.make_async_copy(ref, held.at[p], sems.at[p]).start()
        p = base + lax.rem(at + 2, RING)
        pltpu.make_async_copy(group[3], held.at[p, :, pl.ds(0, cut)], sems.at[p]).start()
        rest = held.shape[2] - cut
        pltpu.make_async_copy(group[4], held.at[p, :, pl.ds(cut, rest)], sems.at[p]).start()


def wait_weights(held, sems, p):
    pltpu.make_async_copy(held.at[p], held.at[p], sems.at[p]).wait()


def split_rows(value, scratch, core, p, keep_ref, send_ref):
    scratch[:, :BLK] = value
    for z in range(RING):
        keep_ref[z, p] = scratch[pl.ds(pl.multiple_of(core * 128 + 32 * z, 32), 32), :]
        send_ref[z, p] = scratch[pl.ds(pl.multiple_of((1 - core) * 128 + 32 * z, 32), 32), :].astype(
            LOW
        )


def join_rows(is_low, own, got):
    return jnp.concatenate(
        [jnp.where(is_low, own, got), jnp.where(is_low, got, own)], axis=0
    )


def rope(values, cosine, sine):
    half = HD // 2
    turned = jnp.concatenate([-values[:, half:], values[:, :half]], axis=1)
    return values * cosine + turned * sine


def head_probs(query, keys, mask):
    scores = dot(query, keys, 1, 1) * HD ** (-0.5)
    scores = jnp.where(mask, scores, NEG_BIG)
    weight = jnp.exp(scores - jnp.max(scores, axis=1, keepdims=True))
    return weight / jnp.sum(weight, axis=1, keepdims=True)


def causal_mask(seg_col, seg_row):
    rows = lax.broadcasted_iota(jnp.int32, (SEQ, SEQ), 0)
    cols = lax.broadcasted_iota(jnp.int32, (SEQ, SEQ), 1)
    return (seg_col == seg_row) & (cols <= rows)


def attention_kernel(
    meta_ref, own_ref, got_ref, cos_ref, sin_ref, segc_ref, segr_ref, *rest
):
    w_refs = rest[:10]
    q_ref, k_ref, v_ref, o_ref, keep_ref, send_ref, held, acc, part, sems = rest[10:]
    core = meta_ref[0]
    is_low = core == 0
    start_weights(meta_ref, w_refs, held, sems, CUT)
    acc[...] = jnp.zeros_like(acc)
    part[:, BLK:] = jnp.zeros((SEQ, LANES - BLK), F32)

    def project(p, carry):
        wait_weights(held, sems, p)
        rows = join_rows(is_low, own_ref[p, :128], got_ref[p, :128])
        acc[...] += dot(rows[:, :BLK], held[p, :, 256:], 1, 0)
        return carry

    lax.fori_loop(0, PIECES, project, 0)
    cosine = cos_ref[...]
    sine = sin_ref[...]
    mask = causal_mask(segc_ref[...], segr_ref[...])
    projected = acc[...]
    keys = rope(projected[:, 384:464], cosine, sine).astype(LOW)
    values = projected[:, 464:544].astype(LOW)
    k_ref[...] = keys
    v_ref[...] = values
    outs = []
    for h in range(HEADS):
        query = rope(projected[:, 64 + h * HD : 64 + (h + 1) * HD], cosine, sine).astype(LOW)
        q_ref[h] = query
        probs = head_probs(query, keys, mask)
        outs.append(dot(probs.astype(LOW), values, 1, 0))
    outs.append(jnp.zeros((SEQ, 64), F32))
    attended = jnp.concatenate(outs, axis=1).astype(LOW)
    o_ref[...] = attended

    def spread(p, carry):
        split_rows(dot(attended, held[p, :, :384], 1, 1), part, core, p, keep_ref, send_ref)
        return carry

    lax.fori_loop(0, PIECES, spread, 0)


def split_shapes():
    return [
        jax.ShapeDtypeStruct((RING, PIECES, 32, LANES), F32),
        jax.ShapeDtypeStruct((RING, PIECES, 32, LANES), LOW),
    ]


def attention_forward(meta, own, got, tables, segs, w_attn):
    return pl.pallas_call(
        attention_kernel,
        in_specs=[smem()] + [whole()] * 6 + [hbm()] * 10,
        out_specs=[whole()] * 6,
        out_shape=[
            jax.ShapeDtypeStruct((HEADS, SEQ, HD), LOW),
            jax.ShapeDtypeStruct((SEQ, HD), LOW),
            jax.ShapeDtypeStruct((SEQ, HD), LOW),
            jax.ShapeDtypeStruct((SEQ, 384), LOW),
        ]
        + split_shapes(),
        scratch_shapes=[
            pltpu.VMEM((PIECES, BLK, ATTN), LOW),
            pltpu.VMEM((SEQ, ATTN - 256), F32),
            pltpu.VMEM((SEQ, LANES), F32),
            pltpu.SemaphoreType.DMA((PIECES,)),
        ],
        compiler_params=pltpu.CompilerParams(vmem_limit_bytes=VMEM),
        cost_estimate=cost(0, 0),
        name="attention_forward",
    )(meta, own, got, *tables, *segs, *w_attn)


def attention_back_kernel(
    meta_ref, own_ref, got_ref, cos_ref, sin_ref, segc_ref, segr_ref, q_ref, k_ref, v_ref, *rest
):
    w_refs = rest[:10]
    right_ref, keep_ref, send_ref, held, acc, part, sems = rest[10:]
    core = meta_ref[0]
    is_low = core == 0
    start_weights(meta_ref, w_refs, held, sems, CUT)
    acc[...] = jnp.zeros_like(acc)
    part[:, BLK:] = jnp.zeros((SEQ, LANES - BLK), F32)

    def project(p, carry):
        wait_weights(held, sems, p)
        own = jnp.concatenate([own_ref[z, p] for z in range(RING)], axis=0)
        got = jnp.concatenate([got_ref[z, p] for z in range(RING)], axis=0)
        acc[...] += dot(join_rows(is_low, own, got)[:, :BLK], held[p, :, :384], 1, 0)
        return carry

    lax.fori_loop(0, PIECES, project, 0)
    cosine = cos_ref[...]
    sine = -sin_ref[...]
    mask = causal_mask(segc_ref[...], segr_ref[...])
    grad_att = acc[...]
    keys = k_ref[...]
    values = v_ref[...]
    factor = HD ** (-0.5)
    grads = []
    grad_keys = jnp.zeros((SEQ, HD), F32)
    grad_values = jnp.zeros((SEQ, HD), F32)
    for h in range(HEADS):
        query = q_ref[h]
        grad_o = grad_att[:, h * HD : (h + 1) * HD].astype(LOW)
        probs = head_probs(query, keys, mask)
        grad_probs = dot(grad_o, values, 1, 1)
        inner = jnp.sum(probs * grad_probs, axis=1, keepdims=True)
        grad_scores = (probs * (grad_probs - inner)).astype(LOW)
        grads.append(rope(dot(grad_scores, keys, 1, 0) * factor, cosine, sine))
        grad_keys += dot(grad_scores, query, 0, 0)
        grad_values += dot(probs.astype(LOW), grad_o, 0, 0)
    grads.append(rope(grad_keys * factor, cosine, sine))
    grads.append(grad_values)
    zeros = [jnp.zeros((SEQ, 64), F32)]
    ends = [jnp.zeros((SEQ, 96), F32)]
    grad_qkv = jnp.concatenate(zeros + grads + ends, axis=1).astype(LOW)
    right_ref[...] = grad_qkv

    def spread(p, carry):
        split_rows(dot(grad_qkv, held[p, :, 256:], 1, 1), part, core, p, keep_ref, send_ref)
        return carry

    lax.fori_loop(0, PIECES, spread, 0)


def attention_backward(meta, own, got, tables, segs, qkv, w_attn):
    return pl.pallas_call(
        attention_back_kernel,
        in_specs=[smem()] + [whole()] * 9 + [hbm()] * 10,
        out_specs=[whole()] * 3,
        out_shape=[jax.ShapeDtypeStruct((SEQ, ATTN - 256), LOW)] + split_shapes(),
        scratch_shapes=[
            pltpu.VMEM((PIECES, BLK, ATTN), LOW),
            pltpu.VMEM((SEQ, 384), F32),
            pltpu.VMEM((SEQ, LANES), F32),
            pltpu.SemaphoreType.DMA((PIECES,)),
        ],
        compiler_params=pltpu.CompilerParams(vmem_limit_bytes=VMEM),
        cost_estimate=cost(0, 0),
        name="attention_backward",
    )(meta, own, got, *tables, *segs, *qkv, *w_attn)


def start_ffn(meta_ref, refs, held, sems):
    x = meta_ref[2]
    y = meta_ref[3]
    for base, at, group in ((0, y, refs[:13]), (RING, x, refs[13:])):
        for k, offset in enumerate((0, -1, 1)):
            p = base + lax.rem(at + offset + RING, RING)
            for j in range(3):
                into = held.at[p, :, pl.ds(j * FW, FW)]
                pltpu.make_async_copy(group[3 * k + j], into, sems.at[p]).start()
        p = base + lax.rem(at + 2, RING)
        spans = ((0, FW), (FW, CUT), (FW + CUT, FW - CUT), (2 * FW, FW))
        for ref, (start, width) in zip(group[9:], spans):
            pltpu.make_async_copy(ref, held.at[p, :, pl.ds(start, width)], sems.at[p]).start()


def ffn_kernel(meta_ref, own_ref, got_ref, cot_own_ref, cot_got_ref, *rest):
    w_refs = rest[:26]
    act_ref, grad_ref, keep_ref, send_ref, mkeep_ref, msend_ref, held, acc, part, sems = rest[26:]
    core = meta_ref[0]
    is_low = core == 0
    start_ffn(meta_ref, w_refs, held, sems)
    acc[...] = jnp.zeros_like(acc)
    part[:, BLK:] = jnp.zeros((SEQ, LANES - BLK), F32)

    def project(p, carry):
        wait_weights(held, sems, p)
        own = jnp.concatenate([own_ref[z, p] for z in range(RING)], axis=0)
        got = jnp.concatenate([got_ref[z, p] for z in range(RING)], axis=0)
        rows = join_rows(is_low, own, got)
        cot = join_rows(is_low, cot_own_ref[p, 128:], cot_got_ref[p, 128:])
        acc[:, :FW] += dot(cot[:, :BLK], held[p, :, :FW], 1, 0)
        acc[:, FW:] += dot(rows[:, :BLK], held[p, :, FW:], 1, 0)
        return carry

    lax.fori_loop(0, PIECES, project, 0)

    def units(t, carry):
        at = pl.multiple_of(t * 128, 128)
        grad_act = acc[:, pl.ds(at, 128)]
        gate = acc[:, pl.ds(at + FW, 128)]
        up = acc[:, pl.ds(at + 2 * FW, 128)]
        sigmoid = 1.0 / (1.0 + jnp.exp(-gate))
        silu = gate * sigmoid
        act_ref[:, pl.ds(at, 128)] = (silu * up).astype(LOW)
        grad_gate = grad_act * up * sigmoid * (1.0 + gate * (1.0 - sigmoid))
        grad_ref[:, pl.ds(at, 128)] = grad_gate.astype(LOW)
        grad_ref[:, pl.ds(at + FW, 128)] = (grad_act * silu).astype(LOW)
        return carry

    lax.fori_loop(0, FW // 128, units, 0)

    def spread(p, carry):
        split_rows(dot(grad_ref[...], held[p, :, FW:], 1, 1), part, core, p, keep_ref, send_ref)
        split_rows(dot(act_ref[...], held[p, :, :FW], 1, 1), part, core, p, mkeep_ref, msend_ref)
        return carry

    lax.fori_loop(0, PIECES, spread, 0)


def feed_forward(meta, own, got, cot_own, cot_got, w_ffn):
    return pl.pallas_call(
        ffn_kernel,
        in_specs=[smem()] + [whole()] * 4 + [hbm()] * 26,
        out_specs=[whole()] * 6,
        out_shape=[
            jax.ShapeDtypeStruct((SEQ, FW), LOW),
            jax.ShapeDtypeStruct((SEQ, 2 * FW), LOW),
        ]
        + split_shapes()
        + split_shapes(),
        scratch_shapes=[
            pltpu.VMEM((PIECES, BLK, FFN), LOW),
            pltpu.VMEM((SEQ, FFN), F32),
            pltpu.VMEM((SEQ, LANES), F32),
            pltpu.SemaphoreType.DMA((PIECES,)),
        ],
        compiler_params=pltpu.CompilerParams(vmem_limit_bytes=VMEM),
        cost_estimate=cost(0, 0),
        name="feed_forward",
    )(meta, own, got, cot_own, cot_got, *w_ffn)


def halves_of(part_ref, xc_ref, q, at):
    rows = jnp.concatenate([part_ref[z, q] for z in range(RING)], axis=0)
    return rows[:, :BLK], xc_ref[q, at : at + 128][:, :BLK]


def terms_kernel(meta_ref, own_ref, got_ref, xc_ref, xc_got_ref, *rest, attn, wanted):
    is_low = meta_ref[0] == 0
    rights = rest[:2]
    outs = rest[2:-1]
    acc = rest[-1]
    passed = len(wanted) == 2
    count = 4 if passed else (2 if wanted == (3,) else 1)
    if passed:
        far_refs, outs = outs[:4], outs[4:]
    for kind in range(2):
        at = meta_ref[3 - kind]
        group = outs[kind * count : kind * count + count]
        for n, k in enumerate(wanted):
            q = kind * RING + lax.rem(at + OFFSETS[k] + RING, RING)
            own_part, own_xc = halves_of(own_ref, xc_ref, q, 0 if attn else 128)
            got_part, got_xc = halves_of(got_ref, xc_got_ref, q, 0 if attn else 128)
            part = join_rows(is_low, own_part, got_part)
            xc = join_rows(is_low, own_xc, got_xc)
            if attn:
                one = dot(part, rights[0][...], 0, 0)
                two = dot(xc, rights[1][...], 0, 0)
                acc[...] = jnp.concatenate([one[:, :QW], two[:, 64:]], axis=1)
            else:
                acc[:, :FW] = dot(xc, rights[0][...], 0, 0)
                acc[:, FW:] = dot(part, rights[1][...], 0, 0)
            cut = CUT if attn else FFN_CUT
            if passed and k == 1:
                acc[:, cut:] += far_refs[2 * kind + 1][...].astype(F32)
            if passed and k == 2:
                acc[:, :cut] += far_refs[2 * kind][...].astype(F32)
            if wanted == (0,):
                group[0][...] = acc[...].astype(LOW)
            else:
                group[2 * n][...] = acc[:, :cut].astype(LOW)
                group[2 * n + 1][...] = acc[:, cut:].astype(LOW)


def weight_terms(meta, parts, xcs, rights, wanted, fars=()):
    attn = rights[0].shape[1] == 384
    width = ATTN if attn else FFN
    cut = CUT if attn else FFN_CUT
    if wanted == (0,):
        shapes = [(BLK, width)] * 2
    else:
        shapes = [(BLK, cut), (BLK, width - cut)] * (2 * len(wanted))
    return pl.pallas_call(
        functools.partial(terms_kernel, attn=attn, wanted=wanted),
        in_specs=[smem()] + [whole()] * (6 + len(fars)),
        out_specs=[whole()] * len(shapes),
        out_shape=[jax.ShapeDtypeStruct(shape, LOW) for shape in shapes],
        scratch_shapes=[pltpu.VMEM((BLK, width), F32)],
        compiler_params=pltpu.CompilerParams(vmem_limit_bytes=VMEM),
        cost_estimate=cost(0, 0),
        name="terms_attention" if attn else "terms_feed_forward",
    )(meta, *parts, *xcs, *rights, *fars)


def middle_kernel(*refs):
    for kind in range(2):
        attn = refs[5 * kind : 5 * kind + 5]
        ffn = refs[10 + 5 * kind : 15 + 5 * kind]
        own_ref, back_ref, ahead_ref, one_ref, two_ref = refs[20 + 5 * kind : 25 + 5 * kind]

        def total(own, nears, start, stop, first, last):
            value = own[first:last, start:stop].astype(F32)
            for n in nears:
                value = value + n[first:last].astype(F32)
            return value

        for k, ref in enumerate((own_ref, back_ref, ahead_ref, None)):
            first = k * HALF
            last = first + HALF
            parts = (
                (0, total(attn[0], (attn[1], attn[3]), 0, CUT, first, last)),
                (CUT, total(attn[0], (attn[2], attn[4]), CUT, ATTN, first, last)),
                (ATTN, total(ffn[0], (ffn[1], ffn[3]), 0, FFN_CUT, first, last)),
                (ATTN + FFN_CUT, total(ffn[0], (ffn[2], ffn[4]), FFN_CUT, FFN, first, last)),
            )
            for start, value in parts:
                stop = start + value.shape[1]
                if ref is not None:
                    ref[:, start:stop] = value
                elif stop <= WIDE_CUT:
                    one_ref[:, start:stop] = value.astype(LOW)
                elif start >= WIDE_CUT:
                    two_ref[:, start - WIDE_CUT : stop - WIDE_CUT] = value.astype(LOW)
                else:
                    cut = WIDE_CUT - start
                    one_ref[:, start:] = value[:, :cut].astype(LOW)
                    two_ref[:, : stop - WIDE_CUT] = value[:, cut:].astype(LOW)


def middle(attn, ffn):
    args = []
    for group in (attn, ffn):
        for kind in range(2):
            own, nears = group[kind]
            args += [own, *nears]
    shapes = [jax.ShapeDtypeStruct((HALF, WIDE), F32)] * 3
    shapes += [jax.ShapeDtypeStruct((HALF, WIDE_CUT), LOW)] * 2
    outs = pl.pallas_call(
        middle_kernel,
        in_specs=[whole()] * 20,
        out_specs=[whole()] * 10,
        out_shape=shapes * 2,
        compiler_params=pltpu.CompilerParams(vmem_limit_bytes=VMEM),
        cost_estimate=cost(0, 0),
        name="middle",
    )(*args)
    return outs[:5], outs[5:]


def add_far_kernel(*refs):
    for kind in range(2):
        back, ahead, one, two = refs[4 * kind : 4 * kind + 4]
        up, down = refs[8 + 2 * kind : 10 + 2 * kind]
        cut = one.shape[1]
        up[:, :cut] = (ahead[:, :cut] + one[...].astype(F32)).astype(LOW)
        up[:, cut:] = ahead[:, cut:].astype(LOW)
        down[:, :cut] = back[:, :cut].astype(LOW)
        down[:, cut:] = (back[:, cut:] + two[...].astype(F32)).astype(LOW)


def add_far(terms, fars):
    width = terms[0][0].shape[1]
    args = []
    for t, f in zip(terms, fars):
        args += [t[1], t[2], *f]
    outs = pl.pallas_call(
        add_far_kernel,
        in_specs=[whole()] * 8,
        out_specs=[whole()] * 4,
        out_shape=[jax.ShapeDtypeStruct((HALF, width), LOW)] * 4,
        compiler_params=pltpu.CompilerParams(vmem_limit_bytes=VMEM),
        cost_estimate=cost(0, 0),
        name="add_far",
    )(*args)
    return outs[:2], outs[2:]


def finish_kernel(meta_ref, *refs):
    is_low = meta_ref[0] == 0
    sums = []
    for kind in range(2):
        own, one, two = refs[3 * kind : 3 * kind + 3]
        sums.append(own[...] + one[...].astype(F32) + two[...].astype(F32))
    stay_ref, send_ref = refs[6:]
    stay_ref[...] = jnp.where(is_low, sums[0], sums[1])
    send_ref[...] = jnp.where(is_low, sums[1], sums[0]).astype(LOW)


def finish(meta, terms, nears):
    width = terms[0][0].shape[1]
    args = []
    for t, n in zip(terms, nears):
        args += [t[0], *n]
    return pl.pallas_call(
        finish_kernel,
        in_specs=[smem()] + [whole()] * 6,
        out_specs=[whole()] * 2,
        out_shape=[
            jax.ShapeDtypeStruct((HALF, width), F32),
            jax.ShapeDtypeStruct((HALF, width), LOW),
        ],
        compiler_params=pltpu.CompilerParams(vmem_limit_bytes=VMEM),
        cost_estimate=cost(0, 0),
        name="finish",
    )(meta, *args)


def adam_kernel(meta_ref, w_ref, m_ref, v_ref, stay, came, wo_ref, mo_ref, vo_ref, grad):
    is_low = meta_ref[0] == 0
    rows = w_ref.shape[0]
    for start, at, width in MAP:
        mine = stay[:, at : at + width]
        other = came[:, at : at + width]
        grad[:, start : start + width] = jnp.where(is_low, mine, other)
        grad[:, start + width : start + 2 * width] = jnp.where(is_low, other, mine)
    row = pl.program_id(0) * rows + lax.broadcasted_iota(jnp.int32, (rows, 1), 0)
    valid = row < meta_ref[4]
    weight, first, second = adam_step(
        w_ref[...], m_ref[...], v_ref[...], grad[...], LEARN, DECAY
    )
    wo_ref[...] = jnp.where(valid, weight, 0.0)
    mo_ref[...] = jnp.where(valid, first, 0.0)
    vo_ref[...] = jnp.where(valid, second, 0.0)


def adam(meta, master, moment_one, moment_two, stay, came):
    rows = 24
    units = master.shape[1]

    def block(width):
        return pl.BlockSpec((rows, width), lambda i: (i, 0))

    return pl.pallas_call(
        adam_kernel,
        grid=(HALF // rows,),
        in_specs=[smem()] + [block(units)] * 3 + [block(WIDE)] * 2,
        out_specs=[block(units)] * 3,
        out_shape=[jax.ShapeDtypeStruct(master.shape, F32)] * 3,
        scratch_shapes=[pltpu.VMEM((rows, units), F32)],
        compiler_params=pltpu.CompilerParams(vmem_limit_bytes=VMEM),
        name="adam",
    )(meta, master, moment_one, moment_two, stay, came)


def rms_scale(values):
    return lax.rsqrt(jnp.sum(values * values, axis=(0, 2), keepdims=True) / D + EPS_NORM)


def rms_backward(grad_out, normed, scale, gain):
    grad_normed = grad_out * gain
    inner = jnp.sum(grad_normed * normed, axis=(0, 2), keepdims=True) / D
    return scale * (grad_normed - normed * inner), jnp.sum(grad_out * normed, axis=1)


def adam_step(weight, first, second, grad, rate, decay):
    first_new = BETA * first + (1.0 - BETA) * grad
    second_new = BETA * second + (1.0 - BETA) * grad * grad
    correction = 1.0 - BETA**STEP
    update = first_new / correction / (jnp.sqrt(second_new / correction) + EPS_ADAM)
    return (weight - rate * (update + decay * weight), first_new, second_new)


def stage(*values):
    return lax.optimization_barrier(values)


def shards(
    tokens, cotangent, segments, owner, master, moment_one, moment_two, gains, gain_one, gain_two
):
    core = lax.axis_index("core")
    yl = lax.axis_index("yl")
    z = lax.axis_index("z")
    x = lax.axis_index(X)
    y = lax.axis_index("yh") * 2 + yl
    count = jnp.sum((owner == (y // 2 * RING + x) * 2 + core).astype(jnp.int32)) - yl * HALF
    meta = jnp.stack([core, z, x, y, count]).astype(jnp.int32)
    along = (Y, X)
    across = (X, Y)

    def add_core(keep, other):
        return (keep + other.astype(F32)).astype(LOW)

    def split_z(block):
        return lax.all_to_all(block, "z", split_axis=0, concat_axis=0, tiled=True)

    def sum_z(block):
        return jnp.sum(block.astype(F32), axis=0)

    def all_z(block):
        return split_z(jnp.broadcast_to(block[None], (RING, *block.shape)))

    own, send = pack(meta, master)
    got = swap_core(send)
    numbers = jnp.zeros((8, D), LOW).at[0, :SEQ].set(segments.astype(LOW))
    swapped = swap_sequences(jnp.concatenate([tokens, cotangent, numbers], axis=0))
    first = jnp.where(core == 0, own, got)
    second = jnp.where(core == 0, got, own)
    first, second, swapped, owner = stage(first, second, swapped, owner)

    near_first = near(first, X)
    near_second = near(second, Y)
    onehot = (owner[:, None] == jnp.arange(16, dtype=jnp.int32)[None, :]).astype(jnp.int32)
    rank = jnp.sum((jnp.cumsum(onehot, axis=0) - onehot) * onehot, axis=1)
    slot = (owner * CAP + rank)[:, None]
    ids = slot_ids(x, y)
    segment = swapped[256, :SEQ].astype(jnp.int32)
    segs = (segment[:, None], segment[None, :])
    parts = jnp.concatenate([three_parts(gains), jnp.zeros((10, D), LOW)], axis=0)
    xc_own, inputs, cot_z, gain = to_slots(meta, slot, ids, swapped, gains, parts)
    near_first, near_second, xc_own, inputs, cot_z, gain, segs = stage(
        near_first, near_second, xc_own, inputs, cot_z, gain, segs
    )

    far_first = halves(*near_first, X, WIDE_CUT)
    far_second = halves(*near_second, Y, WIDE_CUT)
    xc_got = swap_core(xc_own)
    far_first, far_second, xc_got = stage(far_first, far_second, xc_got)
    blocks = assemble(first, *near_first, *far_first, second, *near_second, *far_second)
    attn, down, gate, up = ([blocks[j], blocks[4 + j]] for j in range(4))

    attn_near = [near(b, axis) for b, axis in zip(attn, along)]
    position = jnp.arange(SEQ, dtype=F32)
    freq = jnp.exp(-jnp.log(THETA) * (2.0 * jnp.arange(HD // 2, dtype=F32) / HD))
    angle = position[:, None] * freq[None, :]
    tables = (
        jnp.concatenate([jnp.cos(angle)] * 2, axis=1),
        jnp.concatenate([jnp.sin(angle)] * 2, axis=1),
    )
    attn_near, tables = stage(attn_near, tables)
    attn_far = [halves(*n, axis, CUT) for n, axis in zip(attn_near, along)]
    attn_far, down = stage(attn_far, down)
    w_attn = (attn[0], *attn_near[0], *attn_far[0], attn[1], *attn_near[1], *attn_far[1])

    down_near = [near(b, axis) for b, axis in zip(down, along)]
    *qkv, attended, keep, send = attention_forward(meta, xc_own, xc_got, tables, segs, w_attn)
    down_near, gate, keep, send = stage(down_near, gate, keep, send)

    gate_near = [near(b, axis) for b, axis in zip(gate, along)]
    got = split_z(add_core(keep, swap_core(send)))
    gate_near, up, got = stage(gate_near, up, got)

    up_near = [near(b, axis) for b, axis in zip(up, along)]
    hidden = inputs + sum_z(got)
    scale_two = rms_scale(hidden)
    normed_two = hidden * scale_two
    xn_two = all_z((normed_two * gain[:, 1:2]).astype(LOW))
    xn_two_got = swap_core(xn_two)
    gate_cut = [(n[0][:, :CUT], n[1][:, CUT:]) for n in gate_near]
    up_near, down_near, gate_cut, xn_two, xn_two_got = stage(
        up_near, down_near, gate_cut, xn_two, xn_two_got
    )

    far_ends = [far(d[0], u[1], axis) for d, u, axis in zip(down_near, up_near, along)]
    far_ends, gate_cut = stage(far_ends, gate_cut)
    gate_far = [far(*g, axis) for g, axis in zip(gate_cut, along)]
    gate_far, xn_two = stage(gate_far, xn_two)
    w_ffn = []
    for kind in range(2):
        own_blocks = (down[kind], gate[kind], up[kind])
        nears = (down_near[kind], gate_near[kind], up_near[kind])
        w_ffn += [*own_blocks, *(n[0] for n in nears), *(n[1] for n in nears)]
        w_ffn += [far_ends[kind][0], *gate_far[kind], far_ends[kind][1]]

    act, grad_gu, keep, send, keep_mlp, send_mlp = feed_forward(
        meta, xn_two, xn_two_got, xc_own, xc_got, w_ffn
    )
    xn_twos = (xn_two, xn_two_got)
    xcs = (xc_own, xc_got)
    ffn_fars = weight_terms(meta, xn_twos, xcs, (act, grad_gu), (3,))
    send_got = swap_core(send)
    ffn_fars, send_got = stage(ffn_fars, send_got)
    ffn_fars = [far(*ffn_fars[2 * k : 2 * k + 2], axis) for k, axis in enumerate(along)]
    got = split_z(add_core(keep, send_got))
    ffn_own = weight_terms(meta, xn_twos, xcs, (act, grad_gu), (0,))
    ffn_fars, got, ffn_own, send_mlp = stage(ffn_fars, got, ffn_own, send_mlp)

    def sends(terms, part):
        return [
            (move(terms[4 * k + 2 + part], axis, 1), move(terms[4 * k + part], axis, -1))
            for k, axis in enumerate(along)
        ]

    ffn_terms = weight_terms(
        meta, xn_twos, xcs, (act, grad_gu), (1, 2), (*ffn_fars[0], *ffn_fars[1])
    )
    ffn_one = sends(ffn_terms, 0)
    grad_xn_two = sum_z(got)
    grad_norm_two, gain_grad_two = rms_backward(grad_xn_two, normed_two, scale_two, gain[:, 1:2])
    grad_hidden = cot_z + grad_norm_two
    grad_branch = all_z(grad_hidden.astype(LOW))
    grad_branch_got = swap_core(grad_branch)
    ffn_one, ffn_terms, grad_branch, grad_branch_got, send_mlp = stage(
        ffn_one, ffn_terms, grad_branch, grad_branch_got, send_mlp
    )

    ffn_two = sends(ffn_terms, 1)
    grad_qkv, keep, send = attention_backward(
        meta, grad_branch, grad_branch_got, tables, segs, qkv, w_attn
    )
    branches = (grad_branch, grad_branch_got)
    attn_fars = weight_terms(meta, branches, xcs, (attended, grad_qkv), (3,))
    attn_own = weight_terms(meta, branches, xcs, (attended, grad_qkv), (0,))
    mlp_got = swap_core(send_mlp)
    ffn_two, attn_fars, attn_own, keep, send, mlp_got = stage(
        ffn_two, attn_fars, attn_own, keep, send, mlp_got
    )
    attn_fars = [far(*attn_fars[2 * k : 2 * k + 2], axis) for k, axis in enumerate(along)]
    send_got = swap_core(send)
    attn_fars, send_got, mlp_got = stage(attn_fars, send_got, mlp_got)
    attn_terms = weight_terms(
        meta, branches, xcs, (attended, grad_qkv), (1, 2), (*attn_fars[0], *attn_fars[1])
    )
    attn_one = [
        (move(attn_terms[4 * k + 2], axis, 1), move(attn_terms[4 * k], axis, -1))
        for k, axis in enumerate(along)
    ]
    got = split_z(add_core(keep, send_got))
    attn_one, attn_terms, got, mlp_got = stage(attn_one, attn_terms, got, mlp_got)
    attn_two = sends(attn_terms, 1)
    grad_xn_one = sum_z(got)
    scale_one = rms_scale(inputs)
    grad_norm_one, gain_grad_one = rms_backward(
        grad_xn_one, inputs * scale_one, scale_one, gain[:, 0:1]
    )
    grad_tokens_z = (grad_hidden + grad_norm_one).astype(LOW)
    got_mlp = split_z(add_core(keep_mlp, mlp_got))
    attn_two, grad_tokens_z, gain_grad_one, got_mlp = stage(
        attn_two, grad_tokens_z, gain_grad_one, got_mlp
    )

    def both(own, one, two):
        return [(own[k], (one[k][0], two[k][0], one[k][1], two[k][1])) for k in range(2)]

    blocks = middle(both(attn_own, attn_one, attn_two), both(ffn_own, ffn_one, ffn_two))
    fars = [far(b[3], b[4], axis) for b, axis in zip(blocks, across)]
    output_z = (hidden + sum_z(got_mlp)).astype(LOW)
    gain_grads = three_parts(jnp.stack([gain_grad_one, gain_grad_two], axis=0))
    gain_grads = jnp.swapaxes(gain_grads, 0, 1)
    blank = jnp.zeros((PIECES, 10, LANES), LOW)
    last = from_slots(
        jnp.concatenate([output_z, grad_tokens_z, gain_grads, blank], axis=1), slot, ids
    )
    fars, blocks, last = stage(fars, blocks, last)
    nears = [
        (move(up, axis, 1), move(down, axis, -1))
        for (up, down), axis in zip(add_far(blocks, fars), across)
    ]
    part = lax.all_gather(last.astype(LOW), "z", axis=0, tiled=False)
    nears, blocks, part = stage(nears, blocks, part)
    stay, send = finish(meta, blocks, nears)
    came = swap_core(send).astype(F32)
    moved = swap_sequences(jnp.swapaxes(part[:, :64].reshape(RING, 2, 32, D), 0, 1))
    output = moved[0].reshape(128, D)
    grad_tokens = moved[1].reshape(128, D)

    gain_grads = part[:, 64:70].astype(F32).sum(axis=0)
    gain_grads = gain_grads[:2] + gain_grads[2:4] + gain_grads[4:6]
    gain_grads = gain_grads + swap_core(gain_grads)

    def sum_along(value, axis, at):
        back, ahead = near(value, axis)
        blocks = (value, back, ahead, move(back, axis, 1))
        every = jnp.zeros((RING, *value.shape), F32)
        for offset, block in zip(OFFSETS, blocks):
            every = lax.dynamic_update_slice_in_dim(every, block[None], (at + offset) % RING, 0)
        return jnp.sum(every, axis=0)

    gain_grads = sum_along(sum_along(gain_grads, X, x), Y, y)
    new_gains, new_gain_one, new_gain_two = adam_step(
        gains, gain_one, gain_two, gain_grads, LEARN_GAIN, 0.0
    )
    new_master, new_one, new_two = adam(meta, master, moment_one, moment_two, stay, came)
    return (
        output,
        grad_tokens,
        new_master,
        new_one,
        new_two,
        new_gains,
        new_gain_one,
        new_gain_two,
    )


def solution(mesh):
    fine = Mesh(mesh.devices.reshape(2, 4, 2, 2, 4), ("yh", "x", "core", "yl", "z"))
    rows = ("yh", "x", "core", "yl")
    in_specs = (
        P(rows, None),
        P(rows, None),
        P(("yh", "x", "core")),
        P(),
        P(rows, "z"),
        P(rows, "z"),
        P(rows, "z"),
        P(),
        P(),
        P(),
    )
    out_specs = (
        P(rows, None),
        P(rows, None),
        P(rows, "z"),
        P(rows, "z"),
        P(rows, "z"),
        P(),
        P(),
        P(),
    )
    return jax.shard_map(shards, mesh=fine, in_specs=in_specs, out_specs=out_specs, check_vma=False)
```

time: 1950 us -> 599 us (0.31)
  blocking collectives: 857 us -> 15.4 us
  local copies, waits for them, and re-layouts: 538 us -> 25.3 us
  waiting for transfers between devices: 361 us -> 188 us
  Pallas kernels: 0 us -> 159 us
  starting transfers between devices: 17.8 us -> 152 us
  matrix products: 106 us -> 0 us
  other arithmetic: 56 us -> 33.2 us
    psum x1 -> x0, blocking collectives: 857 us -> none  [shards(): lax.psum(jnp.stack([gain_grad_one, gain_grad_two]), ('fsdp', 'ctx'))]
    scatter x3 -> x0, local copies, waits for them, and re-layouts: 386 us -> none  [the longest x2 376 us: unpack(): return carry.at[slot_feature].set(piece, mode='drop')]
    all_gather x1, waiting for transfers between devices: 273 us -> 6.99 us  [shards(): part = lax.all_gather(last.astype(LOW), 'z', axis=0, tiled=False)]
    ppermute x4 -> x86, waiting for transfers between devices: 1.09 us -> 170 us  [the longest x74 158 us: move(): return lax.ppermute(block, axis, route)]
    pallas_call x0 -> x17, Pallas kernels: none -> 159 us  [the longest x6 37.7 us: weight_terms(): pl.pallas_call(functools.partial(terms_kernel, attn=attn, wanted=wanted),...]
    ppermute x4 -> x86, starting transfers between devices: 6.17 us -> 132 us  [the longest x74 101 us: move(): return lax.ppermute(block, axis, route)]
    concatenate x2 -> x1, local copies, waits for them, and re-layouts: 106 us -> 0.08 us  [shards(): jnp.concatenate([output_z, grad_tokens_z, gain_grads, blank], axis=1)]
    dot_general x17 -> x0, matrix products: 104 us -> none  [the longest x8 66.7 us: contract(): lax.dot_general(left, right, (((left_axis,), (right_axis,)), ((), ())), p...]
  transfers between devices with their start and end apart: 10 -> 92, of which waited for: 5 -> 42; matrix products, arithmetic and copies ran while one was open for 6% -> 6% of each run, Pallas kernels for 0% -> 19%
where the time goes in v1:
time: 599 us; the launch traced here: 589 us
  waiting for transfers between devices  188 us (31%)
  Pallas kernels  159 us (27%)
  starting transfers between devices  152 us (25%)
  other arithmetic  33.2 us (6%)
  local copies, waits for them, and re-layouts  25.3 us (4%)
  between operations  16.1 us (3%)
  blocking collectives  15.4 us (3%)
    ppermute x74, waiting for transfers between devices, move(): return lax.ppermute(block, axis, route)  158 us
    ppermute x74, starting transfers between devices, move(): return lax.ppermute(block, axis, route)  101 us
    pallas_call x6, Pallas kernels, weight_terms(): pl.pallas_call(functools.partial(terms_kernel, attn=attn, wanted=wanted),...  37.7 us
    pallas_call x1, Pallas kernels, feed_forward(): pl.pallas_call(ffn_kernel, in_specs=[smem()] + [whole()] * 4 + [hbm()] *...  24.2 us
    ppermute x10, starting transfers between devices, swap_core(): return lax.ppermute(block, 'core', [(0, 1), (1, 0)])  24 us
    all_to_all x5, starting transfers between devices, split_z(): return lax.all_to_all(block, 'z', split_axis=0, concat_axis=0, tiled=True)  20.2 us
    all_to_all x1, blocking collectives, split_z(): return lax.all_to_all(block, 'z', split_axis=0, concat_axis=0, tiled=True)  15.4 us
    pallas_call x1, Pallas kernels, attention_forward(): pl.pallas_call(attention_kernel, in_specs=[smem()] + [whole()] * 6 + [hbm...  14.2 us
  transfers between devices with their start and end apart: 92, of which 42 were waited for; matrix products, arithmetic and copies ran while one was open for 6% of the time, Pallas kernels for 19%

profile of v1, /device:TPU:1, one launch (start us, length us, event | category | flops | bytes accessed | tf_op | source)
XLA Modules:
  0.0 588.9 jit_solution(14429870990268912016)
XLA Ops:
  9.8 4.2 pack.1
  16.7 3.2 collective-permute-start.1
  24.1 12.3 %collective-permute-done.1.swapped_ref = bf16[264,2560]{1,0:T(8,128)(2,1)} collective-permute-done((bf16[264,2560]{1,0:T(8,128)(2,1)}, bf16[264,2560]{1,0:T(8,128)(2,1)}, u32[]{:S(2)}, u32[]{:S(2)}) %collective-permute-start.1) | collective-permute-done | bytes 1351712 | tf_op jit(solution)/shard_map/ppermute | solution.py:75
  41.8 4.6 reduce-window.6
  49.2 12.3 %to_slots.1 = (bf16[8,256,512]{2,1,0:T(8,128)(2,1)}, f32[8,32,512]{2,1,0:T(8,128)}, f32[8,32,512]{2,1,0:T(8,128)}, f32[8,2,512]{2,1,0:T(2,128)}) custom-call(s32[5]{0:T(128)} %stack.32.meta_ref, s32[2560,1]{1,0:T(8,128)} %broadcast_in_dim.72.slot_ref, s32[8,1,512]{2,1,0:T(1,128)} %pad.10.ids_ref, bf16[264,2560]{1,0:T(8,128)(2,1)} %collective-permute-done.1.swapped_ref, ...), custom_call_target="tpu_custom_call" | custom-call | tf_op jit(solution)/shard_map/to_slots/pallas_call | solution.py:205
  72.6 4.0 collective-permute-done.6.refs_3_
  76.7 4.2 collective-permute-done.8.refs_8_
  82.5 7.1 %assemble.1 = (bf16[480,896]{1,0:T(8,128)(2,1)}, bf16[480,896]{1,0:T(8,128)(2,1)}, bf16[480,896]{1,0:T(8,128)(2,1)}, bf16[480,896]{1,0:T(8,128)(2,1)}, bf16[480,...) custom-call(bf16[120,3584]{1,0:T(8,128)(2,1)} %copy-done.11, ...), custom_call_target="tpu_custom_call" | custom-call | tf_op jit(solution)/shard_map/assemble/pallas_call | solution.py:165
  96.5 13.7 %collective-permute-done.11.rest_1_ = bf16[480,896]{1,0:T(8,128)(2,1)S(1)} collective-permute-done((bf16[480,896]{1,0:T(8,128)(2,1)}, bf16[480,896]{1,0:T(8,128)(2,1)S(1)}, u32[]{:S(2)}, u32[]{:S(2)}) %collective-permute-start.11) | collective-permute-done | bytes 860192 | tf_op jit(solution)/shard_map/ppermute | solution.py:67
  112.7 3.2 collective-permute-start.16
  130.2 14.2 %attention_forward.1 = (bf16[4,256,80]{2,1,0:T(8,128)(2,1)}, bf16[256,80]{1,0:T(8,128)(2,1)}, bf16[256,80]{1,0:T(8,128)(2,1)}, bf16[256,384]{1,0:T(8,128)(2,1)},...) custom-call(s32[5]{0:T(128)} %stack.32.meta_ref, ...), custom_call_target="tpu_custom_call" | custom-call | tf_op jit(solution)/shard_map/attention_forward/pallas_call | solution.py:359
  145.3 5.5 collective-permute-start.27
  159.1 5.2 all-to-all-start
  164.9 8.2 %collective-permute-done.23.rest_4_ = bf16[480,896]{1,0:T(8,128)(2,1)S(1)} collective-permute-done((bf16[480,896]{1,0:T(8,128)(2,1)}, bf16[480,896]{1,0:T(8,128)(2,1)S(1)}, u32[]{:S(2)}, u32[]{:S(2)}) %collective-permute-start.23) | collective-permute-done | bytes 860192 | tf_op jit(solution)/shard_map/ppermute | solution.py:67
  179.1 15.4 %all_to_all.30.own_ref = bf16[4,8,32,512]{3,2,1,0:T(8,128)(2,1)S(1)} all-to-all(bf16[4,8,32,512]{3,2,1,0:T(8,128)(2,1)S(1)} %broadcast_in_dim.25), channel_id=1, replica_groups=mesh['yh'=2,'x'=4,'core'=2,'yl'=2,'z'=4] {'z'}, dimensions={0} | all-to-all | bytes 2097152 | tf_op jit(solution)/shard_map/all_to_all | solution.py:786
  194.5 3.2 collective-permute-start.32
  206.3 13.3 %collective-permute-done.28.rest_5_ = bf16[480,896]{1,0:T(8,128)(2,1)S(1)} collective-permute-done((bf16[480,896]{1,0:T(8,128)(2,1)S(1)}, bf16[480,896]{1,0:T(8,128)(2,1)S(1)}, u32[]{:S(2)}, u32[]{:S(2)}) %collective-permute-start.28) | collective-permute-done | bytes 860192 | tf_op jit(solution)/shard_map/ppermute | solution.py:67
  227.1 15.0 %collective-permute-done.33.rest_9_ = bf16[480,896]{1,0:T(8,128)(2,1)S(1)} collective-permute-done((bf16[480,896]{1,0:T(8,128)(2,1)S(1)}, bf16[480,896]{1,0:T(8,128)(2,1)S(1)}, u32[]{:S(2)}, u32[]{:S(2)}) %collective-permute-start.33) | collective-permute-done | bytes 860192 | tf_op jit(solution)/shard_map/ppermute | solution.py:67
  256.4 24.2 %feed_forward.1 = (bf16[256,896]{1,0:T(8,128)(2,1)}, bf16[256,1792]{1,0:T(8,128)(2,1)}, f32[4,8,32,512]{3,2,1,0:T(8,128)}, bf16[4,8,32,512]{3,2,1,0:T(8,128)(2,1...) custom-call(s32[5]{0:T(128)} %stack.32.meta_ref, bf16[4,8,32,512]{3,2,1,0:T(8,128)(2,1)} %copy-done.1, ...), custom_call_target="tpu_custom_call" | custom-call | tf_op jit(solution)/shard_map/feed_forward/pallas_call | solution.py:513
  280.5 4.4 collective-permute-start.41
  284.9 6.2 %terms_feed_forward.3 = (bf16[480,1408]{1,0:T(8,128)(2,1)}, bf16[480,1280]{1,0:T(8,128)(2,1)}, bf16[480,1408]{1,0:T(8,128)(2,1)}, bf16[480,1280]{1,0:T(8,128)(2,1)}) custom-call(s32[5]{0:T(128)} %stack.32.meta_ref, bf16[4,8,32,512]{3,2,1,0:T(8,128)(2,1)} %copy-done.1, bf16[4,8,32,512]{3,2,1,0:T(8,128)(2,1)} %copy-done.3, ...), custom_call_target="tpu_custom_call" | custom-call | tf_op jit(solution)/shard_map/terms_feed_forward/pallas_call | solution.py:585
  300.0 3.5 all-to-all-start.2
  303.5 6.5 %terms_feed_forward.4 = (bf16[480,2688]{1,0:T(8,128)(2,1)}, bf16[480,2688]{1,0:T(8,128)(2,1)}) custom-call(s32[5]{0:T(128)} %stack.32.meta_ref, bf16[4,8,32,512]{3,2,1,0:T(8,128)(2,1)} %copy-done.1, bf16[4,8,32,512]{3,2,1,0:T(8,128)(2,1)} %copy-done.3, bf16[8,256,512]{2,1,0:T(8,128)(2,1)} %get-tuple-element.261.own_ref.cot_own_ref.xc_ref, ...), custom_call_target="tpu_custom_call" | custom-call | tf_op jit(solution)/shard_map/terms_feed_forward/pallas_call | solution.py:585
  310.0 7.8 %all-to-all-done.2 = bf16[4,8,32,512]{3,2,1,0:T(8,128)(2,1)S(1)} async-done(((bf16[4,8,32,512]{3,2,1,0:T(8,128)(2,1)}), bf16[4,8,32,512]{3,2,1,0:T(8,128)(2,1)S(1)}, u32[]{:S(2)}, u32[]{:S(2)}) %all-to-all-start.2) | async-done | bytes 1048608 | tf_op jit(solution)/shard_map/all_to_all | solution.py:786
  317.7 3.4 collective-permute-done.43.rest_3_
  321.1 3.1 collective-permute-done.45.rest_5_
  328.2 3.5 all-to-all-start.3
  331.7 9.8 %terms_feed_forward.5 = (bf16[480,1408]{1,0:T(8,128)(2,1)}, bf16[480,1280]{1,0:T(8,128)(2,1)}, bf16[480,1408]{1,0:T(8,128)(2,1)}, bf16[480,1280]{1,0:T(8,128)(2,...) custom-call(s32[5]{0:T(128)} %stack.32.meta_ref, ...), custom_call_target="tpu_custom_call" | custom-call | tf_op jit(solution)/shard_map/terms_feed_forward/pallas_call | solution.py:585
  348.8 24.7 %collective-permute-done.46.refs_11_ = bf16[480,1408]{1,0:T(8,128)(2,1)} collective-permute-done((bf16[480,1408]{1,0:T(8,128)(2,1)}, bf16[480,1408]{1,0:T(8,128)(2,1)}, u32[]{:S(2)}, u32[]{:S(2)}) %collective-permute-start.46) | collective-permute-done | bytes 1351712 | tf_op jit(solution)/shard_map/ppermute | solution.py:67
  381.3 3.3 collective-permute-start.55
  384.5 13.3 %attention_backward.1 = (bf16[256,640]{1,0:T(8,128)(2,1)}, f32[4,8,32,512]{3,2,1,0:T(8,128)}, bf16[4,8,32,512]{3,2,1,0:T(8,128)(2,1)}) custom-call(s32[5]{0:T(128)} %stack.32.meta_ref, bf16[4,8,32,512]{3,2,1,0:T(8,128)(2,1)} %copy-done.2, bf16[4,8,32,512]{3,2,1,0:T(8,128)(2,1)} %copy-done.4, f32[256,80]{1,0:T(8,128)} %get-tuple-element.279.cos_ref, ...), custom_call_target="tpu_custom_call" | custom-call | tf_op jit(solution)/shard_map/attention_backward/pallas_call | solution.py:436
  397.8 4.8 terms_attention.4
  402.6 4.7 terms_attention.3
  414.9 5.5 collective-permute-done.57.rest_3_
  425.3 4.0 all-to-all-start.4
  429.2 5.7 terms_attention.5
  440.9 7.0 %collective-permute-done.61.refs_1_ = bf16[480,512]{1,0:T(8,128)(2,1)S(1)} collective-permute-done((bf16[480,512]{1,0:T(8,128)(2,1)}, bf16[480,512]{1,0:T(8,128)(2,1)S(1)}, u32[]{:S(2)}, u32[]{:S(2)}) %collective-permute-start.61) | collective-permute-done | bytes 491552 | tf_op jit(solution)/shard_map/ppermute | solution.py:67
  450.9 3.2 add_convert_fusion
  454.1 4.0 all-to-all-start.5
  469.8 11.7 %middle.1 = (f32[120,3584]{1,0:T(8,128)}, f32[120,3584]{1,0:T(8,128)}, f32[120,3584]{1,0:T(8,128)}, bf16[120,1792]{1,0:T(8,128)(2,1)}, bf16[120,1792]{1,0:T(8,12...) custom-call(bf16[480,896]{1,0:T(8,128)(2,1)} %get-tuple-element.386., ...), custom_call_target="tpu_custom_call" | custom-call | tf_op jit(solution)/shard_map/middle/pallas_call | solution.py:640
  488.2 13.0 %from_slots.1 = f32[80,2560]{1,0:T(8,128)} custom-call(s32[2560,1]{1,0:T(8,128)} %broadcast_in_dim.72.slot_ref, s32[8,1,512]{2,1,0:T(1,128)} %pad.10.ids_ref, bf16[8,80,512]{2,1,0:T(8,128)(2,1)} %maximum_maximum_fusion.rows_ref), custom_call_target="tpu_custom_call" | custom-call | tf_op jit(solution)/shard_map/from_slots/pallas_call | solution.py:242
  503.8 5.3 add_far.1
  514.5 10.7 %collective-permute-done.73.refs_1_ = bf16[120,3584]{1,0:T(8,128)(2,1)S(1)} collective-permute-done((bf16[120,3584]{1,0:T(8,128)(2,1)}, bf16[120,3584]{1,0:T(8,128)(2,1)S(1)}, u32[]{:S(2)}, u32[]{:S(2)}) %collective-permute-start.73) | collective-permute-done | bytes 860192 | tf_op jit(solution)/shard_map/ppermute | solution.py:67
  527.3 7.0 %all-gather.3.cloned.1.call-done = bf16[320,2560]{1,0:T(8,128)(2,1)} async-done(((bf16[80,2560]{1,0:T(8,128)(2,1)}), bf16[320,2560]{1,0:T(8,128)(2,1)}) %all-gather.3.cloned.1.call-update) | async-done | bytes 1638416 | tf_op jit(solution)/shard_map/all_gather | solution.py:950
  537.7 4.9 finish.1
  543.9 3.3 collective-permute-start.77
  558.1 4.3 collective-permute-done.83
  569.3 11.4 %adam.1 = (f32[120,6976]{1,0:T(8,128)}, f32[120,6976]{1,0:T(8,128)}, f32[120,6976]{1,0:T(8,128)}) custom-call(s32[5]{0:T(128)} %stack.32.meta_ref, f32[120,6976]{1,0:T(8,128)} %w_ref.1, f32[120,6976]{1,0:T(8,128)} %m_ref.1, f32[120,6976]{1,0:T(8,128)} %v_ref.1, f32[120,3584]{1,0:T(8,128)} %get-tuple-element.469.stay, f32[120,3584]{1,0:T(8,128)} %convert_element_type.112.came), custom_call_target="tpu_custom_call" | custom-call | tf_op jit(solution)/shard_map/adam/pallas_call | solution.py:735
  (408 shorter events, 200.1 us)
Async XLA Ops:
  16.7 19.7 %collective-permute-start.1 = (bf16[264,2560]{1,0:T(8,128)(2,1)}, bf16[264,2560]{1,0:T(8,128)(2,1)}, u32[]{:S(2)}, u32[]{:S(2)}) collective-permute-start(bf16[264,2560]{1,0:T(8,128)(2,1)} %fusion.1), channel_id=1, source_target_pairs={{0,0},{4,8},{8,4},{12,12},{1,1},{5,9},{9,5},{13,13},{2,2},{6,10},{... | collective-permute-start | bytes 4055048 | tf_op jit(solution)/shard_map/ppermute | solution.py:75
  36.4 26.4 %collective-permute-start.2 = (bf16[120,3584]{1,0:T(8,128)(2,1)S(1)}, bf16[120,3584]{1,0:T(8,128)(2,1)S(1)}, u32[]{:S(2)}, u32[]{:S(2)}) collective-permute-start(bf16[120,3584]{1,0:T(8,128)(2,1)S(1)} %get-tuple-element.249.refs_0_), channel_id=1, source_target_pairs={{0,16},{16,32},{32,48},{48,0},{1,17},{17,33},{33,49},{49,1},{2,18}... | collective-permute-start | bytes 2580488 | tf_op jit(solution)/shard_map/ppermute | solution.py:67
  37.8 24.9 %collective-permute-start.3 = (bf16[120,3584]{1,0:T(8,128)(2,1)S(1)}, bf16[120,3584]{1,0:T(8,128)(2,1)}, u32[]{:S(2)}, u32[]{:S(2)}) collective-permute-start(bf16[120,3584]{1,0:T(8,128)(2,1)S(1)} %get-tuple-element.249.refs_0_), channel_id=1, source_target_pairs={{0,48},{16,0},{32,16},{48,32},{1,49},{17,1},{33,17},{49,33},{2,50}... | collective-permute-start | bytes 2580488 | tf_op jit(solution)/shard_map/ppermute | solution.py:67
  39.1 23.7 %collective-permute-start.4 = (bf16[120,3584]{1,0:T(8,128)(2,1)S(1)}, bf16[120,3584]{1,0:T(8,128)(2,1)}, u32[]{:S(2)}, u32[]{:S(2)}) collective-permute-start(bf16[120,3584]{1,0:T(8,128)(2,1)S(1)} %get-tuple-element.250.refs_5_), channel_id=1, source_target_pairs={{0,4},{4,64},{64,68},{68,0},{1,5},{5,65},{65,69},{69,1},{2,6},{6,6... | collective-permute-start | bytes 2580488 | tf_op jit(solution)/shard_map/ppermute | solution.py:67
  39.1 23.7 %collective-permute-start.5 = (bf16[120,3584]{1,0:T(8,128)(2,1)S(1)}, bf16[120,3584]{1,0:T(8,128)(2,1)}, u32[]{:S(2)}, u32[]{:S(2)}) collective-permute-start(bf16[120,3584]{1,0:T(8,128)(2,1)S(1)} %get-tuple-element.250.refs_5_), channel_id=1, source_target_pairs={{0,68},{4,0},{64,4},{68,64},{1,69},{5,1},{65,5},{69,65},{2,70},{6,... | collective-permute-start | bytes 2580488 | tf_op jit(solution)/shard_map/ppermute | solution.py:67
  62.8 19.7 %collective-permute-start.10 = (bf16[8,256,512]{2,1,0:T(8,128)(2,1)}, bf16[8,256,512]{2,1,0:T(8,128)(2,1)S(1)}, u32[]{:S(2)}, u32[]{:S(2)}) collective-permute-start(bf16[8,256,512]{2,1,0:T(8,128)(2,1)} %get-tuple-element.261.own_ref.cot_own_ref.xc_ref), channel_id=1, source_target_pairs={{0,8},{8,0},{1,9},{9,1},{2,10},{10,2},{3,11},{11,3},{4,12},{12,4},... | collective-permute-start | bytes 6291464 | tf_op jit(solution)/shard_map/ppermute | solution.py:71
  89.6 20.6 %collective-permute-start.11 = (bf16[480,896]{1,0:T(8,128)(2,1)}, bf16[480,896]{1,0:T(8,128)(2,1)S(1)}, u32[]{:S(2)}, u32[]{:S(2)}) collective-permute-start(bf16[480,896]{1,0:T(8,128)(2,1)} %get-tuple-element.266.rest_0_), channel_id=1, source_target_pairs={{0,4},{4,64},{64,68},{68,0},{1,5},{5,65},{65,69},{69,1},{2,6},{6,6... | collective-permute-start | bytes 2580488 | tf_op jit(solution)/shard_map/ppermute | solution.py:67
  89.9 20.4 %collective-permute-start.12 = (bf16[480,896]{1,0:T(8,128)(2,1)}, bf16[480,896]{1,0:T(8,128)(2,1)S(1)}, u32[]{:S(2)}, u32[]{:S(2)}) collective-permute-start(bf16[480,896]{1,0:T(8,128)(2,1)} %get-tuple-element.266.rest_0_), channel_id=1, source_target_pairs={{0,68},{4,0},{64,4},{68,64},{1,69},{5,1},{65,5},{69,65},{2,70},{6,... | collective-permute-start | bytes 2580488 | tf_op jit(solution)/shard_map/ppermute | solution.py:67
  92.4 20.0 %collective-permute-start.13 = (bf16[480,896]{1,0:T(8,128)(2,1)}, bf16[480,896]{1,0:T(8,128)(2,1)S(1)}, u32[]{:S(2)}, u32[]{:S(2)}) collective-permute-start(bf16[480,896]{1,0:T(8,128)(2,1)} %get-tuple-element.267.rest_5_), channel_id=1, source_target_pairs={{0,16},{16,32},{32,48},{48,0},{1,17},{17,33},{33,49},{49,1},{2,18}... | collective-permute-start | bytes 2580488 | tf_op jit(solution)/shard_map/ppermute | solution.py:67
  92.5 20.0 %collective-permute-start.14 = (bf16[480,896]{1,0:T(8,128)(2,1)}, bf16[480,896]{1,0:T(8,128)(2,1)S(1)}, u32[]{:S(2)}, u32[]{:S(2)}) collective-permute-start(bf16[480,896]{1,0:T(8,128)(2,1)} %get-tuple-element.267.rest_5_), channel_id=1, source_target_pairs={{0,48},{16,0},{32,16},{48,32},{1,49},{17,1},{33,17},{49,33},{2,50}... | collective-permute-start | bytes 2580488 | tf_op jit(solution)/shard_map/ppermute | solution.py:67
  123.6 20.7 %collective-permute-start.19 = (bf16[480,896]{1,0:T(8,128)(2,1)}, bf16[480,896]{1,0:T(8,128)(2,1)S(1)}, u32[]{:S(2)}, u32[]{:S(2)}) collective-permute-start(bf16[480,896]{1,0:T(8,128)(2,1)} %get-tuple-element.274.rest_0_), channel_id=1, source_target_pairs={{0,4},{4,64},{64,68},{68,0},{1,5},{5,65},{65,69},{69,1},{2,6},{6,6... | collective-permute-start | bytes 2580488 | tf_op jit(solution)/shard_map/ppermute | solution.py:67
  124.1 20.2 %collective-permute-start.20 = (bf16[480,896]{1,0:T(8,128)(2,1)}, bf16[480,896]{1,0:T(8,128)(2,1)}, u32[]{:S(2)}, u32[]{:S(2)}) collective-permute-start(bf16[480,896]{1,0:T(8,128)(2,1)} %get-tuple-element.274.rest_0_), channel_id=1, source_target_pairs={{0,68},{4,0},{64,4},{68,64},{1,69},{5,1},{65,5},{69,65},{2,70},{6,... | collective-permute-start | bytes 2580488 | tf_op jit(solution)/shard_map/ppermute | solution.py:67
  126.3 18.1 %collective-permute-start.21 = (bf16[480,896]{1,0:T(8,128)(2,1)}, bf16[480,896]{1,0:T(8,128)(2,1)}, u32[]{:S(2)}, u32[]{:S(2)}) collective-permute-start(bf16[480,896]{1,0:T(8,128)(2,1)} %get-tuple-element.275.rest_13_), channel_id=1, source_target_pairs={{0,16},{16,32},{32,48},{48,0},{1,17},{17,33},{33,49},{49,1},{2,18}... | collective-permute-start | bytes 2580488 | tf_op jit(solution)/shard_map/ppermute | solution.py:67
  150.8 22.3 %collective-permute-start.23 = (bf16[480,896]{1,0:T(8,128)(2,1)}, bf16[480,896]{1,0:T(8,128)(2,1)S(1)}, u32[]{:S(2)}, u32[]{:S(2)}) collective-permute-start(bf16[480,896]{1,0:T(8,128)(2,1)} %get-tuple-element.289.rest_1_), channel_id=1, source_target_pairs={{0,4},{4,64},{64,68},{68,0},{1,5},{5,65},{65,69},{69,1},{2,6},{6,6... | collective-permute-start | bytes 2580488 | tf_op jit(solution)/shard_map/ppermute | solution.py:67
  150.8 22.3 %collective-permute-start.24 = (bf16[480,896]{1,0:T(8,128)(2,1)}, bf16[480,896]{1,0:T(8,128)(2,1)}, u32[]{:S(2)}, u32[]{:S(2)}) collective-permute-start(bf16[480,896]{1,0:T(8,128)(2,1)} %get-tuple-element.289.rest_1_), channel_id=1, source_target_pairs={{0,68},{4,0},{64,4},{68,64},{1,69},{5,1},{65,5},{69,65},{2,70},{6,... | collective-permute-start | bytes 2580488 | tf_op jit(solution)/shard_map/ppermute | solution.py:67
  153.4 21.6 %collective-permute-start.25 = (bf16[480,896]{1,0:T(8,128)(2,1)}, bf16[480,896]{1,0:T(8,128)(2,1)}, u32[]{:S(2)}, u32[]{:S(2)}) collective-permute-start(bf16[480,896]{1,0:T(8,128)(2,1)} %get-tuple-element.290.rest_14_), channel_id=1, source_target_pairs={{0,16},{16,32},{32,48},{48,0},{1,17},{17,33},{33,49},{49,1},{2,18}... | collective-permute-start | bytes 2580488 | tf_op jit(solution)/shard_map/ppermute | solution.py:67
  153.4 21.6 %collective-permute-start.26 = (bf16[480,896]{1,0:T(8,128)(2,1)}, bf16[480,896]{1,0:T(8,128)(2,1)}, u32[]{:S(2)}, u32[]{:S(2)}) collective-permute-start(bf16[480,896]{1,0:T(8,128)(2,1)} %get-tuple-element.290.rest_14_), channel_id=1, source_target_pairs={{0,48},{16,0},{32,16},{48,32},{1,49},{17,1},{33,17},{49,33},{2,50}... | collective-permute-start | bytes 2580488 | tf_op jit(solution)/shard_map/ppermute | solution.py:67
  159.1 18.9 %all-to-all-start = ((bf16[4,8,32,512]{3,2,1,0:T(8,128)(2,1)}), bf16[4,8,32,512]{3,2,1,0:T(8,128)(2,1)S(1)}, u32[]{:S(2)}, u32[]{:S(2)}) async-start(bf16[4,8,32,512]{3,2,1,0:T(8,128)(2,1)} %add_convert_fusion.3), calls=%async_computation | async-start | bytes 2097152 | tf_op jit(solution)/shard_map/all_to_all | solution.py:786
  194.5 27.2 %collective-permute-start.32 = (bf16[4,8,32,512]{3,2,1,0:T(8,128)(2,1)S(1)}, bf16[4,8,32,512]{3,2,1,0:T(8,128)(2,1)S(1)}, u32[]{:S(2)}, u32[]{:S(2)}) collective-permute-start(bf16[4,8,32,512]{3,2,1,0:T(8,128)(2,1)S(1)} %all_to_all.30.own_ref), channel_id=1, source_target_pairs={{0,8},{8,0},{1,9},{9,1},{2,10},{10,2},{3,11},{11,3},{4,12},{12,4},... | collective-permute-start | bytes 3145736 | tf_op jit(solution)/shard_map/ppermute | solution.py:71
  197.7 21.9 %collective-permute-start.28 = (bf16[480,896]{1,0:T(8,128)(2,1)S(1)}, bf16[480,896]{1,0:T(8,128)(2,1)S(1)}, u32[]{:S(2)}, u32[]{:S(2)}) collective-permute-start(bf16[480,896]{1,0:T(8,128)(2,1)S(1)} %copy-done.26), channel_id=1, source_target_pairs={{0,4},{4,64},{64,68},{68,0},{1,5},{5,65},{65,69},{69,1},{2,6},{6,6... | collective-permute-start | bytes 2580488 | tf_op jit(solution)/shard_map/ppermute | solution.py:67
  197.7 21.9 %collective-permute-start.29 = (bf16[480,896]{1,0:T(8,128)(2,1)S(1)}, bf16[480,896]{1,0:T(8,128)(2,1)S(1)}, u32[]{:S(2)}, u32[]{:S(2)}) collective-permute-start(bf16[480,896]{1,0:T(8,128)(2,1)S(1)} %copy-done.26), channel_id=1, source_target_pairs={{0,68},{4,0},{64,4},{68,64},{1,69},{5,1},{65,5},{69,65},{2,70},{6,... | collective-permute-start | bytes 2580488 | tf_op jit(solution)/shard_map/ppermute | solution.py:67
  200.4 21.2 %collective-permute-start.30 = (bf16[480,896]{1,0:T(8,128)(2,1)S(1)}, bf16[480,896]{1,0:T(8,128)(2,1)S(1)}, u32[]{:S(2)}, u32[]{:S(2)}) collective-permute-start(bf16[480,896]{1,0:T(8,128)(2,1)S(1)} %copy-done.27), channel_id=1, source_target_pairs={{0,16},{16,32},{32,48},{48,0},{1,17},{17,33},{33,49},{49,1},{2,18}... | collective-permute-start | bytes 2580488 | tf_op jit(solution)/shard_map/ppermute | solution.py:67
  200.4 21.2 %collective-permute-start.31 = (bf16[480,896]{1,0:T(8,128)(2,1)S(1)}, bf16[480,896]{1,0:T(8,128)(2,1)S(1)}, u32[]{:S(2)}, u32[]{:S(2)}) collective-permute-start(bf16[480,896]{1,0:T(8,128)(2,1)S(1)} %copy-done.27), channel_id=1, source_target_pairs={{0,48},{16,0},{32,16},{48,32},{1,49},{17,1},{33,17},{49,33},{2,50}... | collective-permute-start | bytes 2580488 | tf_op jit(solution)/shard_map/ppermute | solution.py:67
  221.7 20.4 %collective-permute-start.33 = (bf16[480,896]{1,0:T(8,128)(2,1)S(1)}, bf16[480,896]{1,0:T(8,128)(2,1)S(1)}, u32[]{:S(2)}, u32[]{:S(2)}) collective-permute-start(bf16[480,896]{1,0:T(8,128)(2,1)S(1)} %copy-done.29), channel_id=1, source_target_pairs={{0,4},{4,64},{64,68},{68,0},{1,5},{5,65},{65,69},{69,1},{2,6},{6,6... | collective-permute-start | bytes 2580488 | tf_op jit(solution)/shard_map/ppermute | solution.py:67
  221.8 20.3 %collective-permute-start.34 = (bf16[480,896]{1,0:T(8,128)(2,1)S(1)}, bf16[480,896]{1,0:T(8,128)(2,1)S(1)}, u32[]{:S(2)}, u32[]{:S(2)}) collective-permute-start(bf16[480,896]{1,0:T(8,128)(2,1)S(1)} %collective-permute-done.29.rest_8_), channel_id=1, source_target_pairs={{0,68},{4,0},{64,4},{68,64},{1,69},{5,1},{65,5},{69,65},{2,70},{6,... | collective-permute-start | bytes 2580488 | tf_op jit(solution)/shard_map/ppermute | solution.py:67
  224.4 20.0 %collective-permute-start.35 = (bf16[480,896]{1,0:T(8,128)(2,1)}, bf16[480,896]{1,0:T(8,128)(2,1)S(1)}, u32[]{:S(2)}, u32[]{:S(2)}) collective-permute-start(bf16[480,896]{1,0:T(8,128)(2,1)} %collective-permute-done.21.rest_16_), channel_id=1, source_target_pairs={{0,16},{16,32},{32,48},{48,0},{1,17},{17,33},{33,49},{49,1},{2,18}... | collective-permute-start | bytes 2580488 | tf_op jit(solution)/shard_map/ppermute | solution.py:67
  224.5 19.9 %collective-permute-start.36 = (bf16[480,896]{1,0:T(8,128)(2,1)S(1)}, bf16[480,896]{1,0:T(8,128)(2,1)S(1)}, u32[]{:S(2)}, u32[]{:S(2)}) collective-permute-start(bf16[480,896]{1,0:T(8,128)(2,1)S(1)} %collective-permute-done.31.rest_21_), channel_id=1, source_target_pairs={{0,48},{16,0},{32,16},{48,32},{1,49},{17,1},{33,17},{49,33},{2,50}... | collective-permute-start | bytes 2580488 | tf_op jit(solution)/shard_map/ppermute | solution.py:67
  291.1 33.1 %collective-permute-start.42 = (bf16[480,1408]{1,0:T(8,128)(2,1)}, bf16[480,1408]{1,0:T(8,128)(2,1)}, u32[]{:S(2)}, u32[]{:S(2)}) collective-permute-start(bf16[480,1408]{1,0:T(8,128)(2,1)} %get-tuple-element.342), channel_id=1, source_target_pairs={{0,4},{4,64},{64,68},{68,0},{1,5},{5,65},{65,69},{69,1},{2,6},{6,6... | collective-permute-start | bytes 4055048 | tf_op jit(solution)/shard_map/ppermute | solution.py:67
  291.1 33.9 %collective-permute-start.44 = (bf16[480,1408]{1,0:T(8,128)(2,1)}, bf16[480,1408]{1,0:T(8,128)(2,1)}, u32[]{:S(2)}, u32[]{:S(2)}) collective-permute-start(bf16[480,1408]{1,0:T(8,128)(2,1)} %get-tuple-element.344), channel_id=1, source_target_pairs={{0,16},{16,32},{32,48},{48,0},{1,17},{17,33},{33,49},{49,1},{2,18}... | collective-permute-start | bytes 4055048 | tf_op jit(solution)/shard_map/ppermute | solution.py:67
  292.4 28.7 %collective-permute-start.43 = (bf16[480,1280]{1,0:T(8,128)(2,1)}, bf16[480,1280]{1,0:T(8,128)(2,1)}, u32[]{:S(2)}, u32[]{:S(2)}) collective-permute-start(bf16[480,1280]{1,0:T(8,128)(2,1)} %get-tuple-element.343), channel_id=1, source_target_pairs={{0,68},{4,0},{64,4},{68,64},{1,69},{5,1},{65,5},{69,65},{2,70},{6,... | collective-permute-start | bytes 3686408 | tf_op jit(solution)/shard_map/ppermute | solution.py:67
  295.0 29.2 %collective-permute-start.45 = (bf16[480,1280]{1,0:T(8,128)(2,1)}, bf16[480,1280]{1,0:T(8,128)(2,1)}, u32[]{:S(2)}, u32[]{:S(2)}) collective-permute-start(bf16[480,1280]{1,0:T(8,128)(2,1)} %get-tuple-element.345), channel_id=1, source_target_pairs={{0,48},{16,0},{32,16},{48,32},{1,49},{17,1},{33,17},{49,33},{2,50}... | collective-permute-start | bytes 3686408 | tf_op jit(solution)/shard_map/ppermute | solution.py:67
  328.2 18.8 %all-to-all-start.3 = ((bf16[4,8,32,512]{3,2,1,0:T(8,128)(2,1)}), bf16[4,8,32,512]{3,2,1,0:T(8,128)(2,1)S(1)}, u32[]{:S(2)}, u32[]{:S(2)}) async-start(bf16[4,8,32,512]{3,2,1,0:T(8,128)(2,1)} %broadcast_in_dim.26), calls=%async_computation.3 | async-start | bytes 2097152 | tf_op jit(solution)/shard_map/all_to_all | solution.py:786
  341.5 32.1 %collective-permute-start.46 = (bf16[480,1408]{1,0:T(8,128)(2,1)}, bf16[480,1408]{1,0:T(8,128)(2,1)}, u32[]{:S(2)}, u32[]{:S(2)}) collective-permute-start(bf16[480,1408]{1,0:T(8,128)(2,1)} %get-tuple-element.355), channel_id=1, source_target_pairs={{0,4},{4,64},{64,68},{68,0},{1,5},{5,65},{65,69},{69,1},{2,6},{6,6... | collective-permute-start | bytes 4055048 | tf_op jit(solution)/shard_map/ppermute | solution.py:67
  341.7 31.9 %collective-permute-start.47 = (bf16[480,1408]{1,0:T(8,128)(2,1)}, bf16[480,1408]{1,0:T(8,128)(2,1)}, u32[]{:S(2)}, u32[]{:S(2)}) collective-permute-start(bf16[480,1408]{1,0:T(8,128)(2,1)} %get-tuple-element.356), channel_id=1, source_target_pairs={{0,68},{4,0},{64,4},{68,64},{1,69},{5,1},{65,5},{69,65},{2,70},{6,... | collective-permute-start | bytes 4055048 | tf_op jit(solution)/shard_map/ppermute | solution.py:67
  344.4 31.5 %collective-permute-start.48 = (bf16[480,1408]{1,0:T(8,128)(2,1)}, bf16[480,1408]{1,0:T(8,128)(2,1)}, u32[]{:S(2)}, u32[]{:S(2)}) collective-permute-start(bf16[480,1408]{1,0:T(8,128)(2,1)} %get-tuple-element.357), channel_id=1, source_target_pairs={{0,16},{16,32},{32,48},{48,0},{1,17},{17,33},{33,49},{49,1},{2,18}... | collective-permute-start | bytes 4055048 | tf_op jit(solution)/shard_map/ppermute | solution.py:67
  344.7 31.1 %collective-permute-start.49 = (bf16[480,1408]{1,0:T(8,128)(2,1)}, bf16[480,1408]{1,0:T(8,128)(2,1)}, u32[]{:S(2)}, u32[]{:S(2)}) collective-permute-start(bf16[480,1408]{1,0:T(8,128)(2,1)} %get-tuple-element.358), channel_id=1, source_target_pairs={{0,48},{16,0},{32,16},{48,32},{1,49},{17,1},{33,17},{49,33},{2,50}... | collective-permute-start | bytes 4055048 | tf_op jit(solution)/shard_map/ppermute | solution.py:67
  347.1 28.8 %collective-permute-start.50 = (bf16[4,8,32,512]{3,2,1,0:T(8,128)(2,1)S(1)}, bf16[4,8,32,512]{3,2,1,0:T(8,128)(2,1)S(1)}, u32[]{:S(2)}, u32[]{:S(2)}) collective-permute-start(bf16[4,8,32,512]{3,2,1,0:T(8,128)(2,1)S(1)} %all-to-all-done.3.own_ref), channel_id=1, source_target_pairs={{0,8},{8,0},{1,9},{9,1},{2,10},{10,2},{3,11},{11,3},{4,12},{12,4},... | collective-permute-start | bytes 3145736 | tf_op jit(solution)/shard_map/ppermute | solution.py:71
  375.9 31.5 %collective-permute-start.51 = (bf16[480,1280]{1,0:T(8,128)(2,1)}, bf16[480,1280]{1,0:T(8,128)(2,1)}, u32[]{:S(2)}, u32[]{:S(2)}) collective-permute-start(bf16[480,1280]{1,0:T(8,128)(2,1)} %get-tuple-element.366), channel_id=1, source_target_pairs={{0,4},{4,64},{64,68},{68,0},{1,5},{5,65},{65,69},{69,1},{2,6},{6,6... | collective-permute-start | bytes 3686408 | tf_op jit(solution)/shard_map/ppermute | solution.py:67
  375.9 31.4 %collective-permute-start.52 = (bf16[480,1280]{1,0:T(8,128)(2,1)}, bf16[480,1280]{1,0:T(8,128)(2,1)}, u32[]{:S(2)}, u32[]{:S(2)}) collective-permute-start(bf16[480,1280]{1,0:T(8,128)(2,1)} %get-tuple-element.367), channel_id=1, source_target_pairs={{0,68},{4,0},{64,4},{68,64},{1,69},{5,1},{65,5},{69,65},{2,70},{6,... | collective-permute-start | bytes 3686408 | tf_op jit(solution)/shard_map/ppermute | solution.py:67
  378.6 28.7 %collective-permute-start.53 = (bf16[480,1280]{1,0:T(8,128)(2,1)}, bf16[480,1280]{1,0:T(8,128)(2,1)}, u32[]{:S(2)}, u32[]{:S(2)}) collective-permute-start(bf16[480,1280]{1,0:T(8,128)(2,1)} %get-tuple-element.368), channel_id=1, source_target_pairs={{0,16},{16,32},{32,48},{48,0},{1,17},{17,33},{33,49},{49,1},{2,18}... | collective-permute-start | bytes 3686408 | tf_op jit(solution)/shard_map/ppermute | solution.py:67
  379.3 28.0 %collective-permute-start.54 = (bf16[480,1280]{1,0:T(8,128)(2,1)}, bf16[480,1280]{1,0:T(8,128)(2,1)}, u32[]{:S(2)}, u32[]{:S(2)}) collective-permute-start(bf16[480,1280]{1,0:T(8,128)(2,1)} %get-tuple-element.369), channel_id=1, source_target_pairs={{0,48},{16,0},{32,16},{48,32},{1,49},{17,1},{33,17},{49,33},{2,50}... | collective-permute-start | bytes 3686408 | tf_op jit(solution)/shard_map/ppermute | solution.py:67
  381.3 26.0 %collective-permute-start.55 = (bf16[4,8,32,512]{3,2,1,0:T(8,128)(2,1)}, bf16[4,8,32,512]{3,2,1,0:T(8,128)(2,1)}, u32[]{:S(2)}, u32[]{:S(2)}) collective-permute-start(bf16[4,8,32,512]{3,2,1,0:T(8,128)(2,1)} %get-tuple-element.385), channel_id=1, source_target_pairs={{0,8},{8,0},{1,9},{9,1},{2,10},{10,2},{3,11},{11,3},{4,12},{12,4},... | collective-permute-start | bytes 3145736 | tf_op jit(solution)/shard_map/ppermute | solution.py:71
  425.3 25.6 %all-to-all-start.4 = ((bf16[4,8,32,512]{3,2,1,0:T(8,128)(2,1)}), bf16[4,8,32,512]{3,2,1,0:T(8,128)(2,1)S(1)}, u32[]{:S(2)}, u32[]{:S(2)}) async-start(bf16[4,8,32,512]{3,2,1,0:T(8,128)(2,1)} %add_convert_fusion.1), calls=%async_computation.4 | async-start | bytes 2097152 | tf_op jit(solution)/shard_map/all_to_all | solution.py:786
  458.1 76.1 %all-gather.3.cloned.1.call-start = ((), (), s32[]{:S(2)}) async-start(), calls=%async_computation.6 | async-start | bytes 2048000 | tf_op jit(solution)/shard_map/all_gather | solution.py:950
  481.5 19.6 %collective-permute-start.69 = (bf16[120,1792]{1,0:T(8,128)(2,1)}, bf16[120,1792]{1,0:T(8,128)(2,1)S(1)}, u32[]{:S(2)}, u32[]{:S(2)}) collective-permute-start(bf16[120,1792]{1,0:T(8,128)(2,1)} %get-tuple-element.434), channel_id=1, source_target_pairs={{0,16},{16,32},{32,48},{48,0},{1,17},{17,33},{33,49},{49,1},{2,18}... | collective-permute-start | bytes 1290248 | tf_op jit(solution)/shard_map/ppermute | solution.py:67
  481.6 19.5 %collective-permute-start.70 = (bf16[120,1792]{1,0:T(8,128)(2,1)}, bf16[120,1792]{1,0:T(8,128)(2,1)S(1)}, u32[]{:S(2)}, u32[]{:S(2)}) collective-permute-start(bf16[120,1792]{1,0:T(8,128)(2,1)} %get-tuple-element.435), channel_id=1, source_target_pairs={{0,48},{16,0},{32,16},{48,32},{1,49},{17,1},{33,17},{49,33},{2,50}... | collective-permute-start | bytes 1290248 | tf_op jit(solution)/shard_map/ppermute | solution.py:67
  542.7 25.3 %collective-permute-start.78 = (bf16[120,3584]{1,0:T(8,128)(2,1)}, bf16[120,3584]{1,0:T(8,128)(2,1)S(1)}, u32[]{:S(2)}, u32[]{:S(2)}) collective-permute-start(bf16[120,3584]{1,0:T(8,128)(2,1)} %get-tuple-element.470), channel_id=1, source_target_pairs={{0,8},{8,0},{1,9},{9,1},{2,10},{10,2},{3,11},{11,3},{4,12},{12,4},... | collective-permute-start | bytes 2580488 | tf_op jit(solution)/shard_map/ppermute | solution.py:71
  543.9 36.8 %collective-permute-start.77 = (bf16[2,4,32,2560]{3,2,1,0:T(8,128)(2,1)}, bf16[2,4,32,2560]{3,2,1,0:T(8,128)(2,1)S(1)}, u32[]{:S(2)}, u32[]{:S(2)}) collective-permute-start(bf16[2,4,32,2560]{3,2,1,0:T(8,128)(2,1)} %bitcast.44), channel_id=1, source_target_pairs={{0,0},{4,8},{8,4},{12,12},{1,1},{5,9},{9,5},{13,13},{2,2},{6,10},{... | collective-permute-start | bytes 3932168 | tf_op jit(solution)/shard_map/ppermute | solution.py:75
  (117 other events, 1258.5 us)
Sparse Core Ops, SparseCore 0:
  503.9 30.3 all-gather.2
